TPU v7x, 32 devices: a whole 2x2x4 slice. The times are simulated.
32 devices in a mesh: dp: 4 (over y, x), expert: 8 (over z, core).
Axes of the slice: x: 2, y: 2, z: 4, core: 2. Of those that a mesh axis runs over, the one named last changes fastest.
Arguments:
- tokens: bfloat16 [4096, 4096], P(('dp', 'expert')), may hold values from -6 to 6
- out_grad: bfloat16 [4096, 4096], P(('dp', 'expert')), may hold values from -6 to 6
- expert_ids: int32 [4096, 8], P(('dp', 'expert')), may hold values from 0 to 127, all different within a row; in each aligned block of 128 rows (0 to 127, 128 to 255, ...) at most 9 rows name the same one
- gate_weights: float32 [4096, 8], P(('dp', 'expert')), may hold values from 0.1 to 1
- w_gate: bfloat16 [8, 4096, 1536], P('expert', None, 'dp'), may hold values from -0.09375 to 0.09375
- w_up: bfloat16 [8, 4096, 1536], P('expert', None, 'dp'), may hold values from -0.09375 to 0.09375
- w_down: bfloat16 [8, 1536, 4096], P('expert', 'dp'), may hold values from -0.15625 to 0.15625
Outputs:
- token_grad: bfloat16 [4096, 4096], P(('dp', 'expert'))
- gate_grad: bfloat16 [8, 4096, 1536], P('expert', None, 'dp')
- up_grad: bfloat16 [8, 4096, 1536], P('expert', None, 'dp')
- down_grad: bfloat16 [8, 1536, 4096], P('expert', 'dp')
Inputs may be any that keep to these rules, and one draw needn't show every extreme that they name: `expert_ids`: each row names 8 different experts. Within the rows of one device no expert is named by more than 9 rows, a bound that some block reaches of them.
All inputs are finite; a program needn't handle non-finite values.
Results may differ from a plain program's by a relative error of at most 0.014.
Values may be sent and summed in bfloat16 or wider, within the bound.
A program may use at most 192 MiB of HBM per device.

v0:
```python
import jax
import jax.numpy as jnp
from jax import lax
from jax.sharding import PartitionSpec as P

CAP = 9


def slot_tables(expert_ids, gate_weights, experts, cap):
    tok_rows, choose = expert_ids.shape
    flat = expert_ids.reshape(-1)
    onehot = (flat[:, None] == jnp.arange(experts, dtype=jnp.int32)[None, :]).astype(jnp.int32)
    before = jnp.cumsum(onehot, axis=0) - onehot
    ranked = jnp.sum(before * onehot, axis=1)
    target = jnp.where(flat < experts, flat * cap + ranked, -1).reshape(tok_rows, choose)
    slots = jnp.arange(experts * cap, dtype=jnp.int32)
    hits = slots[:, None, None] == target[None, :, :]
    place = jnp.sum(hits.astype(jnp.float32), axis=2)
    scaled = jnp.sum(jnp.where(hits, gate_weights[None, :, :], jnp.float32(0.0)), axis=2)
    return (place, scaled)


def shards(tokens, out_grad, expert_ids, gate_weights, w_gate, w_up, w_down):
    experts = lax.axis_size("expert")
    groups = lax.axis_size("dp")
    width = tokens.shape[1]
    place, scaled = slot_tables(expert_ids, gate_weights, experts, CAP)
    place_bf = place.astype(jnp.bfloat16)
    send_x = jnp.dot(place_bf, tokens, preferred_element_type=jnp.float32).astype(jnp.bfloat16)
    send_dy = jnp.dot(scaled, out_grad.astype(jnp.float32), precision=lax.Precision.HIGHEST).astype(
        jnp.bfloat16
    )
    send_x = send_x.reshape(experts, CAP, width)
    send_dy = send_dy.reshape(experts, CAP, width)
    got_x, got_dy = (
        lax.all_to_all(send_x, "expert", split_axis=0, concat_axis=0, tiled=True),
        lax.all_to_all(send_dy, "expert", split_axis=0, concat_axis=0, tiled=True),
    )
    all_x, all_dy = (
        lax.all_gather(got_x, "dp", axis=0, tiled=True),
        lax.all_gather(got_dy, "dp", axis=0, tiled=True),
    )
    slot_x = all_x.reshape(-1, width)
    slot_dy = all_dy.reshape(-1, width)
    wg = w_gate[0]
    wu = w_up[0]
    wd = w_down[0]
    gate = jnp.dot(slot_x, wg, preferred_element_type=jnp.float32)
    up = jnp.dot(slot_x, wu, preferred_element_type=jnp.float32)
    sig = jax.nn.sigmoid(gate)
    act = (gate * sig * up).astype(jnp.bfloat16)
    d_act = lax.dot_general(
        slot_dy, wd, (((1,), (1,)), ((), ())), preferred_element_type=jnp.float32
    )
    d_up = (d_act * gate * sig).astype(jnp.bfloat16)
    d_gate = (d_act * up * sig * (1.0 + gate * (1.0 - sig))).astype(jnp.bfloat16)
    over_rows = (((0,), (0,)), ((), ()))
    gate_grad = lax.dot_general(
        slot_x, d_gate, over_rows, preferred_element_type=jnp.float32
    ).astype(jnp.bfloat16)
    up_grad = lax.dot_general(slot_x, d_up, over_rows, preferred_element_type=jnp.float32).astype(
        jnp.bfloat16
    )
    down_grad = lax.dot_general(act, slot_dy, over_rows, preferred_element_type=jnp.float32).astype(
        jnp.bfloat16
    )
    over_units = (((1,), (1,)), ((), ()))
    partial_value = lax.dot_general(d_gate, wg, over_units, preferred_element_type=jnp.float32)
    partial_value = partial_value + lax.dot_general(
        d_up, wu, over_units, preferred_element_type=jnp.float32
    )
    partial_bf = partial_value.astype(jnp.bfloat16).reshape(groups, experts, CAP, width)
    returned = lax.all_to_all(
        lax.all_to_all(partial_bf[:, None], "dp", split_axis=0, concat_axis=1, tiled=True),
        "expert",
        split_axis=2,
        concat_axis=2,
        tiled=True,
    )
    returned = returned.reshape(groups, experts * CAP, width)
    slot_grad = jnp.sum(returned.astype(jnp.float32), axis=0).astype(jnp.bfloat16)
    token_grad = lax.dot_general(place_bf, slot_grad, over_rows, preferred_element_type=jnp.float32)
    return (token_grad.astype(jnp.bfloat16), gate_grad[None], up_grad[None], down_grad[None])


def solution(mesh):
    return jax.shard_map(
        shards,
        mesh=mesh,
        in_specs=(
            P(("dp", "expert"), None),
            P(("dp", "expert"), None),
            P(("dp", "expert"), None),
            P(("dp", "expert"), None),
            P("expert", None, "dp"),
            P("expert", None, "dp"),
            P("expert", "dp", None),
        ),
        out_specs=(
            P(("dp", "expert"), None),
            P("expert", None, "dp"),
            P("expert", None, "dp"),
            P("expert", "dp", None),
        ),
        check_vma=False,
    )
```

profile of v0, /device:TPU:0, one launch (start us, length us, event | category | flops | bytes accessed | tf_op | source)
XLA Modules:
  0.0 263.4 jit_solution(3891427368761900563)
XLA Ops:
  7.2 0.0 copy-start
  7.2 0.0 all-gather.5.cloned.1.call-start
  7.2 0.9 copy.46
  8.2 0.1 eq.43
  8.3 0.1 eq.39
  8.4 2.3 reduce-window.6
  10.6 0.3 slice_reduce_fusion
  10.9 0.2 reduce-window.9
  11.1 0.1 add_bitcast_fusion
  11.2 0.1 reduce_sum.44
  11.3 0.7 add_select_fusion
  12.0 0.9 select_reduce_fusion
  12.9 2.4 convolution_convert_fusion.4
  15.3 2.3 reshape.55
  17.5 32.9 %all_to_all.27 = bf16[8,9,4096]{2,1,0:T(8,128)(2,1)S(1)} all-to-all(bf16[8,9,4096]{2,1,0:T(8,128)(2,1)} %reshape.55), channel_id=1, replica_groups=mesh['dp'=4,'expert'=8] {'expert'}, dimensions={0} | all-to-all | bytes 1179648 | tf_op jit(solution)/shard_map/all_to_all | solution.py:36
  50.5 1.2 copy.51
  51.6 0.0 all-gather.5.cloned.1.call-update
  51.7 0.0 all-gather.3.cloned.1.call-start
  51.7 2.7 %convolution_convert_fusion.5 = bf16[72,4096]{1,0:T(8,128)(2,1)} fusion(f32[72,128]{1,0:T(8,128)S(1)} %get-tuple-element.4, bf16[128,4096]{1,0:T(8,128)(2,1)} %param.8), kind=kOutput, calls=%fused_computation.10 | convolution fusion | flops 453279744 | bytes 1675264 | tf_op jit(solution)/shard_map/dot_general | solution.py:30
  54.4 2.3 reshape.53
  56.7 30.1 %all_to_all.28 = bf16[8,9,4096]{2,1,0:T(8,128)(2,1)S(1)} all-to-all(bf16[8,9,4096]{2,1,0:T(8,128)(2,1)} %reshape.53), channel_id=1, replica_groups=mesh['dp'=4,'expert'=8] {'expert'}, dimensions={0} | all-to-all | bytes 1179648 | tf_op jit(solution)/shard_map/all_to_all | solution.py:37
  86.7 1.2 copy.49
  87.9 0.0 all-gather.3.cloned.1.call-update
  87.9 0.3 all-gather.5.cloned.1.call-done
  88.2 5.1 %copy.52 = bf16[32,9,4096]{2,1,0:T(8,128)(2,1)} copy(bf16[32,9,4096]{2,0,1:T(8,128)(2,1)} %all-gather.5.cloned.1.call-done) | data formatting | bytes 4718592 | tf_op jit(solution)/shard_map/all_gather | solution.py:40
  93.3 4.7 %reshape.56 = bf16[288,4096]{1,0:T(8,128)(2,1)} reshape(bf16[32,9,4096]{2,1,0:T(8,128)(2,1)} %copy.52) | data formatting | bytes 4718592 | tf_op jit(solution)/shard_map/reshape | solution.py:43
  98.0 0.0 copy-done
  98.0 0.0 copy-start.3
  98.0 0.0 copy-start.5
  98.0 4.2 %fusion.6 = f32[288,384]{1,0:T(8,128)} fusion(bf16[288,4096]{1,0:T(8,128)(2,1)} %reshape.56, bf16[1,4096,384]{2,1,0:T(8,128)(2,1)S(1)} %copy-done), kind=kOutput, calls=%fused_computation.13 | convolution fusion | flops 905969664 | bytes 5947392 | tf_op jit(solution)/shard_map/dot_general | solution.py:48
  102.2 0.0 copy-done.3
  102.2 0.0 copy-done.5
  102.2 2.2 fusion.9
  104.4 23.8 %all-gather.3.cloned.1.call-done = bf16[32,9,4096]{2,0,1:T(8,128)(2,1)} async-done(((bf16[8,9,4096]{2,0,1:T(8,128)(2,1)}), bf16[32,9,4096]{2,0,1:T(8,128)(2,1)}) %all-gather.3.cloned.1.call-update) | async-done | bytes 2359312 | tf_op jit(solution)/shard_map/all_gather | solution.py:41
  128.1 5.1 %copy.50 = bf16[32,9,4096]{2,1,0:T(8,128)(2,1)} copy(bf16[32,9,4096]{2,0,1:T(8,128)(2,1)} %all-gather.3.cloned.1.call-done) | data formatting | bytes 4718592 | tf_op jit(solution)/shard_map/all_gather | solution.py:41
  133.2 4.7 %reshape.54 = bf16[288,4096]{1,0:T(8,128)(2,1)} reshape(bf16[32,9,4096]{2,1,0:T(8,128)(2,1)} %copy.50) | data formatting | bytes 4718592 | tf_op jit(solution)/shard_map/reshape | solution.py:44
  138.0 4.2 %multiply_convert_fusion.1 = (bf16[288,384]{1,0:T(8,128)(2,1)S(1)}, bf16[288,384]{1,0:T(8,128)(2,1)S(1)}) fusion(f32[288,384]{1,0:T(8,128)} %fusion.6, f32[288,384]{1,0:T(8,128)} %fusion.9, bf16[288,4096]{1,0:T(8,128)(2,1)} %reshape.54, bf16[1,384,4096]{2,1,0:T(8,128)(2,1)} %param.13), kind=kOutput, calls=%fused_computation.21 | convolution fusion | flops 907407360 | bytes 6832128 | tf_op jit(solution)/shard_map/dot_general | solution.py:52
  142.2 0.0 copy-start.9
  142.2 0.0 copy-start.4
  142.2 1.4 fusion.4
  143.7 0.0 copy-done.9
  143.7 0.5 copy-done.4
  144.2 1.5 fusion
  145.7 2.8 %broadcast_in_dim_reshape.2 = bf16[4,1,8,9,4096]{4,3,2,0,1:T(8,128)(2,1)} reshape(bf16[288,4096]{1,0:T(8,128)(2,1)S(1)} %fusion) | data formatting | bytes 4718592 | tf_op jit(solution)/shard_map/broadcast_in_dim;reshape | solution.py:74
  148.5 3.6 %copy.53 = bf16[4,1,8,9,4096]{4,2,3,1,0:T(8,128)(2,1)S(1)} copy(bf16[4,1,8,9,4096]{4,3,2,0,1:T(8,128)(2,1)} %broadcast_in_dim_reshape.2) | data formatting | bytes 4718592 | tf_op jit(solution)/shard_map/broadcast_in_dim;reshape | solution.py:74
  152.2 30.9 %all_to_all.29 = bf16[4,1,8,9,4096]{4,2,3,1,0:T(8,128)(2,1)S(1)} all-to-all(bf16[4,1,8,9,4096]{4,2,3,1,0:T(8,128)(2,1)S(1)} %copy.53), channel_id=1, replica_groups=mesh['dp'=4,'expert'=8] {'dp'}, dimensions={0} | all-to-all | bytes 4718592 | tf_op jit(solution)/shard_map/all_to_all | solution.py:74
  183.1 3.3 %copy.54 = bf16[1,4,8,9,4096]{4,1,3,0,2:T(4,128)(2,1)} copy(bf16[1,4,8,9,4096]{4,2,3,1,0:T(8,128)(2,1)S(1)} %bitcast.57) | data formatting | bytes 4718592 | tf_op jit(solution)/shard_map/all_to_all | solution.py:74
  186.4 0.0 copy-start.6
  186.4 0.0 copy-start.10
  186.4 4.9 %all-to-all-start.3 = ((bf16[1,4,8,9,4096]{4,1,3,0,2:T(4,128)(2,1)}), bf16[1,4,8,9,4096]{4,1,3,0,2:T(4,128)(2,1)}, u32[]{:S(2)}, u32[]{:S(2)}) async-start(bf16[1,4,8,9,4096]{4,1,3,0,2:T(4,128)(2,1)} %copy.54), calls=%async_computation.3 | async-start | bytes 4718592 | tf_op jit(solution)/shard_map/all_to_all | solution.py:73
  191.3 0.0 copy-done.6
  191.3 0.0 copy-done.10
  191.3 3.8 %fusion.1 = bf16[1,4096,384]{2,1,0:T(8,128)(2,1)} fusion(bf16[288,4096]{1,0:T(8,128)(2,1)S(1)} %copy-done.6, bf16[288,384]{1,0:T(8,128)(2,1)S(1)} %copy-done.10), kind=kOutput, calls=%fused_computation.5 | convolution fusion | flops 907542528 | bytes 5726208 | tf_op jit(solution)/shard_map/dot_general | solution.py:58
  195.1 0.0 copy-start.2
  195.1 3.8 %fusion.2 = bf16[1,4096,384]{2,1,0:T(8,128)(2,1)} fusion(bf16[288,4096]{1,0:T(8,128)(2,1)S(1)} %copy-done.6, bf16[288,384]{1,0:T(8,128)(2,1)S(1)} %get-tuple-element.6), kind=kOutput, calls=%fused_computation.6 | convolution fusion | flops 907542528 | bytes 5726208 | tf_op jit(solution)/shard_map/dot_general | solution.py:61
  198.9 0.0 copy-done.2
  198.9 0.0 copy-done.7
  198.9 0.0 copy-done.8
  198.9 3.5 %fusion.3 = bf16[1,384,4096]{2,1,0:T(8,128)(2,1)} fusion(bf16[288,4096]{1,0:T(8,128)(2,1)S(1)} %copy-done.2, f32[288,384]{1,0:T(8,128)S(1)} %copy-done.8, f32[288,384]{1,0:T(8,128)S(1)} %copy-done.7), kind=kOutput, calls=%fused_computation.7 | convolution fusion | flops 908206080 | bytes 6389760 | tf_op jit(solution)/shard_map/dot_general | solution.py:64
  202.4 43.6 %all-to-all-done.3 = bf16[1,4,8,9,4096]{4,1,3,0,2:T(4,128)(2,1)} async-done(((bf16[1,4,8,9,4096]{4,1,3,0,2:T(4,128)(2,1)}), bf16[1,4,8,9,4096]{4,1,3,0,2:T(4,128)(2,1)}, u32[]{:S(2)}, u32[]{:S(2)}) %all-to-all-start.3) | async-done | bytes 2359328 | tf_op jit(solution)/shard_map/all_to_all | solution.py:73
  246.1 5.7 %reduce_sum.47 = bf16[8,9,4096]{2,1,0:T(8,128)(2,1)} reduce(bf16[1,4,8,9,4096]{4,1,3,0,2:T(4,128)(2,1)} %all-to-all-done.3, bf16[]{:T(256)} %constant.17.clone.1), dimensions={0,1}, to_apply=%region_5.6 | reduce | flops 884736 | bytes 2949122 | tf_op jit(solution)/shard_map/reduce_sum | solution.py:81
  251.8 2.3 reduce_sum.48
  254.1 2.5 convolution_convert_fusion.3
  256.6 0.0 copy-done.1
  (6 shorter events, 0.1 us)
Async XLA Ops:
  7.2 90.8 %copy-start = (bf16[1,4096,384]{2,1,0:T(8,128)(2,1)S(1)}, bf16[1,4096,384]{2,1,0:T(8,128)(2,1)}, u32[]{:S(2)}) copy-start(bf16[1,4096,384]{2,1,0:T(8,128)(2,1)} %param.11) | copy-start | bytes 9437188
  7.2 81.0 %all-gather.5.cloned.1.call-start = ((), (), s32[]{:S(2)}) async-start(), calls=%async_computation.5 | async-start | bytes 2949120 | tf_op jit(solution)/shard_map/all_gather | solution.py:40
  51.7 76.5 %all-gather.3.cloned.1.call-start = ((), (), s32[]{:S(2)}) async-start(), calls=%async_computation.4 | async-start | bytes 2949120 | tf_op jit(solution)/shard_map/all_gather | solution.py:41
  98.0 4.2 %copy-start.3 = (bf16[1,4096,384]{2,1,0:T(8,128)(2,1)S(1)}, bf16[1,4096,384]{2,1,0:T(8,128)(2,1)}, u32[]{:S(2)}) copy-start(bf16[1,4096,384]{2,1,0:T(8,128)(2,1)} %param.12) | copy-start | bytes 9437188
  98.0 4.2 %copy-start.5 = (bf16[288,4096]{1,0:T(8,128)(2,1)S(1)}, bf16[288,4096]{1,0:T(8,128)(2,1)}, u32[]{:S(2)}) copy-start(bf16[288,4096]{1,0:T(8,128)(2,1)} %reshape.56) | copy-start | bytes 7077892
  142.2 1.5 copy-start.9
  142.2 2.0 copy-start.4
  186.4 4.9 %copy-start.6 = (bf16[288,4096]{1,0:T(8,128)(2,1)S(1)}, bf16[288,4096]{1,0:T(8,128)(2,1)}, u32[]{:S(2)}) copy-start(bf16[288,4096]{1,0:T(8,128)(2,1)} %reshape.56) | copy-start | bytes 7077892
  186.4 4.9 %copy-start.10 = (bf16[288,384]{1,0:T(8,128)(2,1)S(1)}, bf16[288,384]{1,0:T(8,128)(2,1)}, u32[]{:S(2)}) copy-start(bf16[288,384]{1,0:T(8,128)(2,1)} %copy-done.9) | copy-start | bytes 663556
  186.4 59.7 %all-to-all-start.3 = ((bf16[1,4,8,9,4096]{4,1,3,0,2:T(4,128)(2,1)}), bf16[1,4,8,9,4096]{4,1,3,0,2:T(4,128)(2,1)}, u32[]{:S(2)}, u32[]{:S(2)}) async-start(bf16[1,4,8,9,4096]{4,1,3,0,2:T(4,128)(2,1)} %copy.54), calls=%async_computation.3 | async-start | bytes 4718592 | tf_op jit(solution)/shard_map/all_to_all | solution.py:73
  195.1 3.8 %copy-start.2 = (bf16[288,4096]{1,0:T(8,128)(2,1)S(1)}, bf16[288,4096]{1,0:T(8,128)(2,1)}, u32[]{:S(2)}) copy-start(bf16[288,4096]{1,0:T(8,128)(2,1)} %reshape.54) | copy-start | bytes 7077892
  195.1 3.8 %copy-start.7 = (f32[288,384]{1,0:T(8,128)S(1)}, f32[288,384]{1,0:T(8,128)}, u32[]{:S(2)}) copy-start(f32[288,384]{1,0:T(8,128)} %fusion.6) | copy-start | bytes 1327108
  195.1 3.8 %copy-start.8 = (f32[288,384]{1,0:T(8,128)S(1)}, f32[288,384]{1,0:T(8,128)}, u32[]{:S(2)}) copy-start(f32[288,384]{1,0:T(8,128)} %fusion.9) | copy-start | bytes 1327108
  198.9 57.7 %copy-start.1 = (bf16[1,4096,384]{2,1,0:T(8,128)(2,1)S(1)}, bf16[1,4096,384]{2,1,0:T(8,128)(2,1)}, u32[]{:S(2)}) copy-start(bf16[1,4096,384]{2,1,0:T(8,128)(2,1)} %param.11) | copy-start | bytes 9437188
Sparse Core Ops, SparseCore 0:
  51.8 36.3 all-gather.4
  90.6 37.4 all-gather.2
where the time goes:
time: 264 us; the launch traced here: 263 us
  blocking collectives  93.9 us (36%)
  waiting for transfers between devices  67.7 us (26%)
  local copies, waits for them, and re-layouts  40.7 us (15%)
  matrix products  32.1 us (12%)
  between operations  14.2 us (5%)
  other arithmetic  9.87 us (4%)
  starting transfers between devices  4.95 us (2%)
    all_to_all x1, waiting for transfers between devices, shards(): lax.all_to_all(lax.all_to_all(partial_bf[:, None], 'dp', split_axis=0, co...  43.6 us
    all_to_all x1, blocking collectives, shards(): lax.all_to_all(send_x, 'expert', split_axis=0, concat_axis=0, tiled=True)  32.9 us
    all_to_all x1, blocking collectives, shards(): lax.all_to_all(partial_bf[:, None], 'dp', split_axis=0, concat_axis=1, ti...  30.9 us
    all_to_all x1, blocking collectives, shards(): lax.all_to_all(send_dy, 'expert', split_axis=0, concat_axis=0, tiled=True)  30.1 us
    all_gather x1, waiting for transfers between devices, shards(): lax.all_gather(got_dy, 'dp', axis=0, tiled=True)  23.8 us
    another operation x2, local copies, waits for them, and re-layouts, shards(): partial_bf[:, None]  6.49 us
    reduce_sum x1, other arithmetic, shards(): jnp.sum(returned.astype(jnp.float32), axis=0).astype(jnp.bfloat16)  5.74 us
  transfers between devices with their start and end apart: 3, of which 3 were waited for; matrix products, arithmetic and copies ran while one was open for 13% of the time, Pallas kernels for 0%

commit v1 on v0

v1 whole, which is shorter than its diff:
```python
import jax
import jax.numpy as jnp
from jax import lax
from jax.sharding import PartitionSpec as P

CAP = 9
MAIN = 8
DP = 4
OVER_ROWS = (((0,), (0,)), ((), ()))
OVER_UNITS = (((1,), (1,)), ((), ()))


def slot_tables(expert_ids, gate_weights, experts):
    tok_rows, choose = expert_ids.shape
    flat = expert_ids.reshape(-1)
    onehot = (flat[:, None] == jnp.arange(experts, dtype=jnp.int32)[None, :]).astype(jnp.int32)
    before = jnp.cumsum(onehot, axis=0) - onehot
    ranked = jnp.sum(before * onehot, axis=1)
    row = jnp.where(ranked < MAIN, flat * MAIN + ranked, experts * MAIN + flat)
    target = jnp.where(flat < experts, row, -1).reshape(tok_rows, choose)
    slots = jnp.arange(experts * CAP, dtype=jnp.int32)
    hits = slots[:, None, None] == target[None, :, :]
    place = jnp.sum(hits.astype(jnp.float32), axis=2)
    scaled = jnp.sum(jnp.where(hits, gate_weights[None, :, :], jnp.float32(0.0)), axis=2)
    return (place, scaled)


def pack(rows):
    blocks = rows.shape[0] // CAP
    width = rows.shape[1]
    main = rows[: blocks * MAIN]
    extra = rows[blocks * MAIN :].reshape(blocks * MAIN, width // MAIN)
    return jnp.concatenate([main, extra], axis=1)


def unpack(packed, width):
    main = packed[:, :width]
    extra = packed[:, width:].reshape(packed.shape[0] // MAIN, width)
    return jnp.concatenate([main, extra], axis=0)


def swap(value, bit):
    return lax.ppermute(value, "dp", [(i, i ^ bit) for i in range(DP)])


def gather(own):
    half = own.shape[1] // 2
    one = swap(own, 1)
    two = swap(own, 2)
    three_a = swap(one[:, :half], 2)
    three_b = swap(two[:, half:], 1)
    return jnp.concatenate([own, one, two, jnp.concatenate([three_a, three_b], axis=1)], axis=0)


def reduce_to_own(parts):
    rows = parts.shape[0] // DP
    half = parts.shape[1] // 2
    f32 = jnp.float32
    p = [parts[r * rows : (r + 1) * rows] for r in range(DP)]

    def way(cols, first, second):
        got = swap(jnp.concatenate([p[first][:, cols], p[3][:, cols]], axis=0), first)
        onward = p[second][:, cols].astype(f32) + got[rows:].astype(f32)
        last = swap(onward.astype(jnp.bfloat16), second)
        return p[0][:, cols].astype(f32) + got[:rows].astype(f32) + last.astype(f32)

    a = way(slice(0, half), 1, 2)
    b = way(slice(half, 2 * half), 2, 1)
    return jnp.concatenate([a, b], axis=1).astype(jnp.bfloat16)


def exchange(packed, experts):
    blocks = packed.reshape(experts, MAIN, -1)
    got = lax.all_to_all(blocks, "expert", split_axis=0, concat_axis=0, tiled=True)
    return got.reshape(packed.shape)


def shards(tokens, out_grad, expert_ids, gate_weights, w_gate, w_up, w_down):
    experts = lax.axis_size("expert")
    width = tokens.shape[1]
    bf16, f32 = jnp.bfloat16, jnp.float32
    place, scaled = slot_tables(expert_ids, gate_weights, experts)
    place_bf = place.astype(bf16)
    send_x = jnp.dot(place_bf, tokens, preferred_element_type=f32).astype(bf16)
    send_dy = jnp.dot(scaled, out_grad.astype(f32), precision=lax.Precision.HIGHEST).astype(bf16)
    slot_x = unpack(gather(exchange(pack(send_x), experts)), width)
    slot_dy = unpack(gather(exchange(pack(send_dy), experts)), width)
    wg = w_gate[0]
    wu = w_up[0]
    wd = w_down[0]
    gate = jnp.dot(slot_x, wg, preferred_element_type=f32)
    up = jnp.dot(slot_x, wu, preferred_element_type=f32)
    sig = jax.nn.sigmoid(gate)
    act = (gate * sig * up).astype(bf16)
    d_act = lax.dot_general(slot_dy, wd, OVER_UNITS, preferred_element_type=f32)
    d_up = (d_act * gate * sig).astype(bf16)
    d_gate = (d_act * up * sig * (1.0 + gate * (1.0 - sig))).astype(bf16)
    partial = lax.dot_general(d_gate, wg, OVER_UNITS, preferred_element_type=f32)
    partial = partial + lax.dot_general(d_up, wu, OVER_UNITS, preferred_element_type=f32)
    slot_grad = reduce_to_own(pack(partial.astype(bf16)))
    gate_grad = lax.dot_general(slot_x, d_gate, OVER_ROWS, preferred_element_type=f32).astype(bf16)
    up_grad = lax.dot_general(slot_x, d_up, OVER_ROWS, preferred_element_type=f32).astype(bf16)
    down_grad = lax.dot_general(act, slot_dy, OVER_ROWS, preferred_element_type=f32).astype(bf16)
    returned = unpack(exchange(slot_grad, experts), width)
    token_grad = lax.dot_general(place_bf, returned, OVER_ROWS, preferred_element_type=f32)
    return (token_grad.astype(bf16), gate_grad[None], up_grad[None], down_grad[None])


def solution(mesh):
    return jax.shard_map(
        shards,
        mesh=mesh,
        in_specs=(
            P(("dp", "expert"), None),
            P(("dp", "expert"), None),
            P(("dp", "expert"), None),
            P(("dp", "expert"), None),
            P("expert", None, "dp"),
            P("expert", None, "dp"),
            P("expert", "dp", None),
        ),
        out_specs=(
            P(("dp", "expert"), None),
            P("expert", None, "dp"),
            P("expert", None, "dp"),
            P("expert", "dp", None),
        ),
        check_vma=False,
    )
```

time: 264 us -> 160 us (0.61)
  blocking collectives: 93.9 us -> 0 us
  starting transfers between devices: 4.95 us -> 30.8 us
  local copies, waits for them, and re-layouts: 40.7 us -> 23.2 us
  between operations: 14.2 us -> 1.06 us
  waiting for transfers between devices: 67.7 us -> 59.4 us
  other arithmetic: 9.87 us -> 17 us
  matrix products: 32.1 us -> 27.4 us
    all_to_all x3 -> x0, blocking collectives: 93.9 us -> none  [the longest x1 32.9 us: shards(): lax.all_to_all(send_x, 'expert', split_axis=0, concat_axis=0, tiled=True)]
    ppermute x0 -> x12, waiting for transfers between devices: none -> 28.1 us  [swap(): return lax.ppermute(value, 'dp', [(i, i ^ bit) for i in range(DP)])]
    all_gather x2 -> x0, waiting for transfers between devices: 24 us -> none  [the longest x1 23.8 us: shards(): lax.all_gather(got_dy, 'dp', axis=0, tiled=True)]
    ppermute x0 -> x12, starting transfers between devices: none -> 15.9 us  [swap(): return lax.ppermute(value, 'dp', [(i, i ^ bit) for i in range(DP)])]
    all_to_all x1 -> x3, waiting for transfers between devices: 43.6 us -> 31.3 us  [exchange(): lax.all_to_all(blocks, 'expert', split_axis=0, concat_axis=0, tiled=True)]
    all_gather x2 -> x0, local copies, waits for them, and re-layouts: 10.2 us -> none  [the longest x1 5.11 us: shards(): lax.all_gather(got_x, 'dp', axis=0, tiled=True)]
    slice x1 -> x14, local copies, waits for them, and re-layouts: 0.28 us -> 10.4 us  [the longest x3 2.41 us: unpack(): main = packed[:, :width]]
    all_to_all x1 -> x3, starting transfers between devices: 4.87 us -> 14.9 us  [exchange(): lax.all_to_all(blocks, 'expert', split_axis=0, concat_axis=0, tiled=True)]
  transfers between devices with their start and end apart: 3 -> 15, of which waited for: 3 -> 9; matrix products, arithmetic and copies ran while one was open for 13% -> 20% of each run, Pallas kernels for 0% -> 0%
where the time goes in v1:
time: 160 us; the launch traced here: 159 us
  waiting for transfers between devices  59.4 us (37%)
  starting transfers between devices  30.8 us (19%)
  matrix products  27.4 us (17%)
  local copies, waits for them, and re-layouts  23.2 us (14%)
  other arithmetic  17 us (11%)
    all_to_all x3, waiting for transfers between devices, exchange(): lax.all_to_all(blocks, 'expert', split_axis=0, concat_axis=0, tiled=True)  31.3 us
    ppermute x12, waiting for transfers between devices, swap(): return lax.ppermute(value, 'dp', [(i, i ^ bit) for i in range(DP)])  28.1 us
    ppermute x12, starting transfers between devices, swap(): return lax.ppermute(value, 'dp', [(i, i ^ bit) for i in range(DP)])  15.9 us
    all_to_all x3, starting transfers between devices, exchange(): lax.all_to_all(blocks, 'expert', split_axis=0, concat_axis=0, tiled=True)  14.9 us
    unnamed x57, local copies, waits for them, and re-layouts  7.71 us
    dot_general x1, matrix products, shards(): lax.dot_general(slot_x, d_gate, OVER_ROWS, preferred_element_type=f32)  5.62 us
    dot_general x1, matrix products, shards(): lax.dot_general(slot_x, d_up, OVER_ROWS, preferred_element_type=f32)  3.8 us
    reshape x3, local copies, waits for them, and re-layouts, unpack(): extra = packed[:, width:].reshape(packed.shape[0] // MAIN, width)  3.58 us
  transfers between devices with their start and end apart: 15, of which 9 were waited for; matrix products, arithmetic and copies ran while one was open for 20% of the time, Pallas kernels for 0%

profile of v1, /device:TPU:0, one launch (start us, length us, event | category | flops | bytes accessed | tf_op | source)
XLA Modules:
  0.0 158.9 jit_solution(3418327058403925865)
XLA Ops:
  0.6 0.9 copy.39
  1.8 2.3 %reduce-window.6 = s32[8,8,128]{2,1,0:T(8,128)S(1)} reduce-window(s32[8,8,128]{2,1,0:T(8,128)S(1)} %fusion.22, s32[]{:T(128)} %constant.3.clone.1), window={size=1x1x128 pad=0_0x0_0x127_0}, to_apply=%region_0.0 | reduce-window | flops 1040384 | bytes 65540 | tf_op jit(solution)/shard_map/reduce-window
  4.7 0.7 select_select_fusion
  5.5 0.9 select_reduce_fusion
  6.3 1.5 convolution_convert_fusion.4
  8.0 0.9 pad_maximum_fusion.6
  8.8 6.3 %all-to-all-start.1 = ((bf16[8,8,4608]{2,1,0:T(8,128)(2,1)}), bf16[8,8,4608]{2,1,0:T(8,128)(2,1)}, u32[]{:S(2)}, u32[]{:S(2)}) async-start(bf16[8,8,4608]{2,1,0:T(8,128)(2,1)} %pad_maximum_fusion.6), calls=%async_computation.1 | async-start | bytes 1179648 | tf_op jit(solution)/shard_map/all_to_all | solution.py:74
  15.1 1.8 %convolution_convert_fusion.5 = bf16[72,4096]{1,0:T(8,128)(2,1)S(1)} fusion(f32[72,128]{1,0:T(8,128)S(1)} %get-tuple-element.4, bf16[128,4096]{1,0:T(8,128)(2,1)} %param.8), kind=kOutput, calls=%fused_computation.10 | convolution fusion | flops 453279744 | bytes 1675264 | tf_op jit(solution)/shard_map/dot_general | solution.py:85
  17.1 0.9 pad_maximum_fusion.5
  17.9 14.1 %all-to-all-done.1 = bf16[8,8,4608]{2,1,0:T(8,128)(2,1)} async-done(((bf16[8,8,4608]{2,1,0:T(8,128)(2,1)}), bf16[8,8,4608]{2,1,0:T(8,128)(2,1)}, u32[]{:S(2)}, u32[]{:S(2)}) %all-to-all-start.1) | async-done | bytes 589856 | tf_op jit(solution)/shard_map/all_to_all | solution.py:74
  32.0 4.2 %all-to-all-start = ((bf16[8,8,4608]{2,1,0:T(8,128)(2,1)}), bf16[8,8,4608]{2,1,0:T(8,128)(2,1)}, u32[]{:S(2)}, u32[]{:S(2)}) async-start(bf16[8,8,4608]{2,1,0:T(8,128)(2,1)} %pad_maximum_fusion.5), calls=%async_computation | async-start | bytes 1179648 | tf_op jit(solution)/shard_map/all_to_all | solution.py:74
  36.2 1.6 collective-permute-start.5
  37.8 1.5 collective-permute-start.4
  39.3 13.7 %all-to-all-done = bf16[8,8,4608]{2,1,0:T(8,128)(2,1)} async-done(((bf16[8,8,4608]{2,1,0:T(8,128)(2,1)}), bf16[8,8,4608]{2,1,0:T(8,128)(2,1)}, u32[]{:S(2)}, u32[]{:S(2)}) %all-to-all-start) | async-done | bytes 589856 | tf_op jit(solution)/shard_map/all_to_all | solution.py:74
  53.0 1.5 collective-permute-start.1
  54.5 1.5 collective-permute-start
  56.0 1.0 slice.144
  57.0 0.6 collective-permute-start.7
  57.6 1.0 slice.143
  59.1 10.3 %collective-permute-done.1 = bf16[64,4608]{1,0:T(8,128)(2,1)S(1)} collective-permute-done((bf16[64,4608]{1,0:T(8,128)(2,1)}, bf16[64,4608]{1,0:T(8,128)(2,1)S(1)}, u32[]{:S(2)}, u32[]{:S(2)}) %collective-permute-start.1) | collective-permute-done | bytes 589856 | tf_op jit(solution)/shard_map/ppermute | solution.py:43
  69.4 0.8 copy-done.5
  70.2 0.7 slice.139
  71.0 1.5 collective-permute-start.3
  72.5 0.8 copy-done.7
  73.3 0.7 slice.138
  74.0 1.5 collective-permute-start.2
  75.5 1.8 %collective-permute-done.7 = bf16[64,2304]{1,0:T(8,128)(2,1)S(1)} collective-permute-done((bf16[64,2304]{1,0:T(8,128)(2,1)S(1)}, bf16[64,2304]{1,0:T(8,128)(2,1)S(1)}, u32[]{:S(2)}, u32[]{:S(2)}) %collective-permute-start.7) | collective-permute-done | bytes 294944 | tf_op jit(solution)/shard_map/ppermute | solution.py:43
  77.3 0.7 copy-done.13
  78.0 0.7 copy-done.14
  78.7 1.6 %maximum_maximum_fusion.2 = bf16[256,512]{1,0:T(8,128)(2,1)} fusion(bf16[64,2304]{1,0:T(8,128)(2,1)S(1)} %collective-permute-done.7, bf16[64,2304]{1,0:T(8,128)(2,1)S(1)} %collective-permute-done.6, bf16[64,4608]{1,0:T(8,128)(2,1)} %collective-permute-done.5, bf16[64,4608]{1,0:T(8,128)(2,1)} %collective-permute-done.4, bf16[64,4608]{1,0:T(8,128)(2,1)} %bitcast.7), kind=kLoop, calls=%fused_computation.48 | loop fusion | flops 1310720 | bytes 2621440 | tf_op jit(solution)/shard_map/slice | solution.py:38
  80.3 1.8 %reshape.79 = bf16[32,4096]{1,0:T(8,128)(2,1)} reshape(bf16[256,512]{1,0:T(8,128)(2,1)} %maximum_maximum_fusion.2) | data formatting | bytes 524288 | tf_op jit(solution)/shard_map/reshape | solution.py:38
  82.1 1.8 %maximum_maximum_fusion.1 = bf16[256,4608]{1,0:T(8,128)(2,1)S(1)} fusion(bf16[64,2304]{1,0:T(8,128)(2,1)} %copy-done.13, bf16[64,2304]{1,0:T(8,128)(2,1)} %copy-done.14, bf16[64,4608]{1,0:T(8,128)(2,1)} %collective-permute-done.5, bf16[64,4608]{1,0:T(8,128)(2,1)} %collective-permute-done.4, bf16[64,4608]{1,0:T(8,128)(2,1)} %bitcast.7), kind=kLoop, calls=%fused_computation.22 | loop fusion | flops 11796480 | bytes 4718592 | tf_op jit(solution)/shard_map/concatenate | solution.py:52
  84.2 0.7 copy-done.25
  84.8 2.2 %fusion.6 = f32[288,384]{1,0:T(8,128)} fusion(bf16[1,4096,384]{2,1,0:T(8,128)(2,1)S(1)} %copy-done, bf16[32,4096]{1,0:T(8,128)(2,1)S(1)} %copy-done.25, bf16[256,4096]{1,0:T(8,128)(2,1)S(1)} %slice.145), kind=kOutput, calls=%fused_computation.13 | convolution fusion | flops 910688256 | bytes 5947392 | tf_op jit(solution)/shard_map/dot_general | solution.py:91
  87.6 2.1 %fusion.9 = f32[288,384]{1,0:T(8,128)} fusion(bf16[1,4096,384]{2,1,0:T(8,128)(2,1)S(1)} %copy-done.9, bf16[32,4096]{1,0:T(8,128)(2,1)S(1)} %copy-done.25, bf16[256,4096]{1,0:T(8,128)(2,1)S(1)} %slice.145), kind=kOutput, calls=%fused_computation.16 | convolution fusion | flops 910688256 | bytes 5947392 | tf_op jit(solution)/shard_map/dot_general | solution.py:92
  89.8 1.6 maximum_maximum_fusion.3
  91.4 1.8 %reshape.77 = bf16[32,4096]{1,0:T(8,128)(2,1)} reshape(bf16[256,512]{1,0:T(8,128)(2,1)} %maximum_maximum_fusion.3) | data formatting | bytes 524288 | tf_op jit(solution)/shard_map/reshape | solution.py:38
  93.1 1.8 %maximum_maximum_fusion = bf16[256,4608]{1,0:T(8,128)(2,1)S(1)} fusion(bf16[64,2304]{1,0:T(8,128)(2,1)S(1)} %collective-permute-done.3, bf16[64,2304]{1,0:T(8,128)(2,1)} %collective-permute-done.2, bf16[64,4608]{1,0:T(8,128)(2,1)} %copy-done.5, bf16[64,4608]{1,0:T(8,128)(2,1)} %copy-done.7, bf16[64,4608]{1,0:T(8,128)(2,1)} %bitcast.3), kind=kLoop, calls=%fused_computation.20 | loop fusion | flops 11796480 | bytes 4718592 | tf_op jit(solution)/shard_map/concatenate | solution.py:52
  96.3 1.4 multiply_convert_fusion.1
  97.8 1.4 fusion.4
  99.9 1.4 fusion
  101.3 0.8 slice.153
  102.1 0.7 copy-done.2
  102.8 1.5 slice.152
  104.3 1.1 reshape.80
  105.4 1.2 pad_maximum_fusion.4
  107.2 1.1 fusion.29
  108.4 1.6 collective-permute-start.8
  109.9 8.8 %collective-permute-done.10 = bf16[128,2304]{1,0:T(8,128)(2,1)S(1)} collective-permute-done((bf16[128,2304]{1,0:T(8,128)(2,1)S(1)}, bf16[128,2304]{1,0:T(8,128)(2,1)S(1)}, u32[]{:S(2)}, u32[]{:S(2)}) %collective-permute-start.10) | collective-permute-done | bytes 589856 | tf_op jit(solution)/shard_map/ppermute | solution.py:43
  118.8 1.6 collective-permute-start.11
  120.3 2.6 %collective-permute-done.8 = bf16[128,2304]{1,0:T(8,128)(2,1)S(1)} collective-permute-done((bf16[128,2304]{1,0:T(8,128)(2,1)S(1)}, bf16[128,2304]{1,0:T(8,128)(2,1)S(1)}, u32[]{:S(2)}, u32[]{:S(2)}) %collective-permute-start.8) | collective-permute-done | bytes 589856 | tf_op jit(solution)/shard_map/ppermute | solution.py:43
  122.9 1.0 add_convert_fusion.3
  124.0 2.0 %collective-permute-start.9 = (bf16[64,2304]{1,0:T(8,128)(2,1)S(1)}, bf16[64,2304]{1,0:T(8,128)(2,1)S(1)}, u32[]{:S(2)}, u32[]{:S(2)}) collective-permute-start(bf16[64,2304]{1,0:T(8,128)(2,1)S(1)} %add_convert_fusion.3), channel_id=1, source_target_pairs={{0,16},{8,24},{16,0},{24,8},{1,17},{9,25},{17,1},{25,9},{2,18},{10... | collective-permute-start | bytes 884744 | tf_op jit(solution)/shard_map/ppermute | solution.py:43
  126.6 4.2 %collective-permute-done.9 = bf16[64,2304]{1,0:T(8,128)(2,1)S(1)} collective-permute-done((bf16[64,2304]{1,0:T(8,128)(2,1)S(1)}, bf16[64,2304]{1,0:T(8,128)(2,1)S(1)}, u32[]{:S(2)}, u32[]{:S(2)}) %collective-permute-start.9) | collective-permute-done | bytes 294944 | tf_op jit(solution)/shard_map/ppermute | solution.py:43
  130.7 1.1 fusion.16
  131.8 0.9 pad_maximum_fusion.8
  132.7 4.4 %all-to-all-start.2 = ((bf16[8,8,4608]{2,1,0:T(8,128)(2,1)}), bf16[8,8,4608]{2,1,0:T(8,128)(2,1)}, u32[]{:S(2)}, u32[]{:S(2)}) async-start(bf16[8,8,4608]{2,1,0:T(8,128)(2,1)} %pad_maximum_fusion.8), calls=%async_computation.2 | async-start | bytes 1179648 | tf_op jit(solution)/shard_map/all_to_all | solution.py:74
  137.1 5.6 %fusion.1 = bf16[1,4096,384]{2,1,0:T(8,128)(2,1)} fusion(bf16[288,384]{1,0:T(8,128)(2,1)S(1)} %copy-done.24, bf16[32,4096]{1,0:T(8,128)(2,1)} %reshape.79, bf16[256,4096]{1,0:T(8,128)(2,1)} %copy-done.11), kind=kOutput, calls=%fused_computation.5 | convolution fusion | flops 912261120 | bytes 5726208 | tf_op jit(solution)/shard_map/dot_general | solution.py:101
  142.8 3.8 %fusion.2 = bf16[1,4096,384]{2,1,0:T(8,128)(2,1)} fusion(bf16[288,384]{1,0:T(8,128)(2,1)S(1)} %copy-done.18, bf16[32,4096]{1,0:T(8,128)(2,1)S(1)} %copy-done.26, bf16[256,4096]{1,0:T(8,128)(2,1)S(1)} %copy-done.12), kind=kOutput, calls=%fused_computation.6 | convolution fusion | flops 912261120 | bytes 5726208 | tf_op jit(solution)/shard_map/dot_general | solution.py:102
  146.6 3.5 %fusion.3 = bf16[1,384,4096]{2,1,0:T(8,128)(2,1)} fusion(bf16[32,4096]{1,0:T(8,128)(2,1)S(1)} %copy-done.16, bf16[256,4096]{1,0:T(8,128)(2,1)S(1)} %copy-done.4, f32[288,384]{1,0:T(8,128)S(1)} %copy-done.22, f32[288,384]{1,0:T(8,128)S(1)} %copy-done.20), kind=kOutput, calls=%fused_computation.7 | convolution fusion | flops 912924672 | bytes 6389760 | tf_op jit(solution)/shard_map/dot_general | solution.py:103
  150.1 3.5 %all-to-all-done.2 = bf16[8,8,4608]{2,1,0:T(8,128)(2,1)} async-done(((bf16[8,8,4608]{2,1,0:T(8,128)(2,1)}), bf16[8,8,4608]{2,1,0:T(8,128)(2,1)}, u32[]{:S(2)}, u32[]{:S(2)}) %all-to-all-start.2) | async-done | bytes 589856 | tf_op jit(solution)/shard_map/all_to_all | solution.py:74
  153.6 0.8 slice.157
  154.5 1.9 %slice.156 = bf16[64,4096]{1,0:T(8,128)(2,1)} slice(bf16[64,4608]{1,0:T(8,128)(2,1)} %bitcast.12), slice={[0:64], [0:4096]} | slice | bytes 1048576 | tf_op jit(solution)/shard_map/slice | solution.py:37
  156.4 2.5 %convolution_convert_fusion.3 = bf16[128,4096]{1,0:T(8,128)(2,1)} fusion(bf16[8,4096]{1,0:T(8,128)(2,1)S(1)} %reshape.82, bf16[64,4096]{1,0:T(8,128)(2,1)} %slice.156, bf16[72,128]{1,0:T(8,128)(2,1)S(1)} %get-tuple-element.5), kind=kOutput, calls=%fused_computation.8 | convolution fusion | flops 77201408 | bytes 1656832 | tf_op jit(solution)/shard_map/dot_general | solution.py:105
  (80 shorter events, 5.8 us)
Async XLA Ops:
  0.6 83.5 %copy-start = (bf16[1,4096,384]{2,1,0:T(8,128)(2,1)S(1)}, bf16[1,4096,384]{2,1,0:T(8,128)(2,1)}, u32[]{:S(2)}) copy-start(bf16[1,4096,384]{2,1,0:T(8,128)(2,1)} %param.11) | copy-start | bytes 9437188
  8.8 23.2 %all-to-all-start.1 = ((bf16[8,8,4608]{2,1,0:T(8,128)(2,1)}), bf16[8,8,4608]{2,1,0:T(8,128)(2,1)}, u32[]{:S(2)}, u32[]{:S(2)}) async-start(bf16[8,8,4608]{2,1,0:T(8,128)(2,1)} %pad_maximum_fusion.6), calls=%async_computation.1 | async-start | bytes 1179648 | tf_op jit(solution)/shard_map/all_to_all | solution.py:74
  32.0 21.0 %all-to-all-start = ((bf16[8,8,4608]{2,1,0:T(8,128)(2,1)}), bf16[8,8,4608]{2,1,0:T(8,128)(2,1)}, u32[]{:S(2)}, u32[]{:S(2)}) async-start(bf16[8,8,4608]{2,1,0:T(8,128)(2,1)} %pad_maximum_fusion.5), calls=%async_computation | async-start | bytes 1179648 | tf_op jit(solution)/shard_map/all_to_all | solution.py:74
  36.2 19.8 %collective-permute-start.5 = (bf16[64,4608]{1,0:T(8,128)(2,1)}, bf16[64,4608]{1,0:T(8,128)(2,1)}, u32[]{:S(2)}, u32[]{:S(2)}) collective-permute-start(bf16[64,4608]{1,0:T(8,128)(2,1)} %bitcast.7), channel_id=1, source_target_pairs={{0,16},{8,24},{16,0},{24,8},{1,17},{9,25},{17,1},{25,9},{2,18},{10... | collective-permute-start | bytes 1769480 | tf_op jit(solution)/shard_map/ppermute | solution.py:43
  37.8 19.8 %collective-permute-start.4 = (bf16[64,4608]{1,0:T(8,128)(2,1)}, bf16[64,4608]{1,0:T(8,128)(2,1)}, u32[]{:S(2)}, u32[]{:S(2)}) collective-permute-start(bf16[64,4608]{1,0:T(8,128)(2,1)} %bitcast.7), channel_id=1, source_target_pairs={{0,8},{8,0},{16,24},{24,16},{1,9},{9,1},{17,25},{25,17},{2,10},{10... | collective-permute-start | bytes 1769480 | tf_op jit(solution)/shard_map/ppermute | solution.py:43
  53.0 16.5 %collective-permute-start.1 = (bf16[64,4608]{1,0:T(8,128)(2,1)}, bf16[64,4608]{1,0:T(8,128)(2,1)S(1)}, u32[]{:S(2)}, u32[]{:S(2)}) collective-permute-start(bf16[64,4608]{1,0:T(8,128)(2,1)} %bitcast.3), channel_id=1, source_target_pairs={{0,16},{8,24},{16,0},{24,8},{1,17},{9,25},{17,1},{25,9},{2,18},{10... | collective-permute-start | bytes 1769480 | tf_op jit(solution)/shard_map/ppermute | solution.py:43
  54.5 18.0 %collective-permute-start = (bf16[64,4608]{1,0:T(8,128)(2,1)}, bf16[64,4608]{1,0:T(8,128)(2,1)S(1)}, u32[]{:S(2)}, u32[]{:S(2)}) collective-permute-start(bf16[64,4608]{1,0:T(8,128)(2,1)} %bitcast.3), channel_id=1, source_target_pairs={{0,8},{8,0},{16,24},{24,16},{1,9},{9,1},{17,25},{25,17},{2,10},{10... | collective-permute-start | bytes 1769480 | tf_op jit(solution)/shard_map/ppermute | solution.py:43
  57.0 20.3 %collective-permute-start.7 = (bf16[64,2304]{1,0:T(8,128)(2,1)S(1)}, bf16[64,2304]{1,0:T(8,128)(2,1)S(1)}, u32[]{:S(2)}, u32[]{:S(2)}) collective-permute-start(bf16[64,2304]{1,0:T(8,128)(2,1)S(1)} %slice.144), channel_id=1, source_target_pairs={{0,8},{8,0},{16,24},{24,16},{1,9},{9,1},{17,25},{25,17},{2,10},{10... | collective-permute-start | bytes 884744 | tf_op jit(solution)/shard_map/ppermute | solution.py:43
  58.6 18.7 %collective-permute-start.6 = (bf16[64,2304]{1,0:T(8,128)(2,1)S(1)}, bf16[64,2304]{1,0:T(8,128)(2,1)S(1)}, u32[]{:S(2)}, u32[]{:S(2)}) collective-permute-start(bf16[64,2304]{1,0:T(8,128)(2,1)S(1)} %slice.143), channel_id=1, source_target_pairs={{0,16},{8,24},{16,0},{24,8},{1,17},{9,25},{17,1},{25,9},{2,18},{10... | collective-permute-start | bytes 884744 | tf_op jit(solution)/shard_map/ppermute | solution.py:43
  69.4 0.8 copy-start.5
  71.0 18.8 %collective-permute-start.3 = (bf16[64,2304]{1,0:T(8,128)(2,1)}, bf16[64,2304]{1,0:T(8,128)(2,1)S(1)}, u32[]{:S(2)}, u32[]{:S(2)}) collective-permute-start(bf16[64,2304]{1,0:T(8,128)(2,1)} %slice.139), channel_id=1, source_target_pairs={{0,8},{8,0},{16,24},{24,16},{1,9},{9,1},{17,25},{25,17},{2,10},{10... | collective-permute-start | bytes 884744 | tf_op jit(solution)/shard_map/ppermute | solution.py:43
  72.5 0.8 copy-start.7
  74.0 15.8 %collective-permute-start.2 = (bf16[64,2304]{1,0:T(8,128)(2,1)}, bf16[64,2304]{1,0:T(8,128)(2,1)}, u32[]{:S(2)}, u32[]{:S(2)}) collective-permute-start(bf16[64,2304]{1,0:T(8,128)(2,1)} %slice.138), channel_id=1, source_target_pairs={{0,16},{8,24},{16,0},{24,8},{1,17},{9,25},{17,1},{25,9},{2,18},{10... | collective-permute-start | bytes 884744 | tf_op jit(solution)/shard_map/ppermute | solution.py:43
  77.3 0.7 copy-start.13
  78.0 0.7 copy-start.14
  83.9 1.0 copy-start.25
  84.8 2.2 %copy-start.11 = (bf16[256,4096]{1,0:T(8,128)(2,1)}, bf16[256,4096]{1,0:T(8,128)(2,1)S(1)}, u32[]{:S(2)}) copy-start(bf16[256,4096]{1,0:T(8,128)(2,1)S(1)} %slice.145) | copy-start | bytes 6291460
  84.8 2.8 %copy-start.9 = (bf16[1,4096,384]{2,1,0:T(8,128)(2,1)S(1)}, bf16[1,4096,384]{2,1,0:T(8,128)(2,1)}, u32[]{:S(2)}) copy-start(bf16[1,4096,384]{2,1,0:T(8,128)(2,1)} %param.12) | copy-start | bytes 9437188
  87.6 2.2 %copy-start.6 = (bf16[64,4608]{1,0:T(8,128)(2,1)S(1)}, bf16[64,4608]{1,0:T(8,128)(2,1)}, u32[]{:S(2)}) copy-start(bf16[64,4608]{1,0:T(8,128)(2,1)} %copy-done.5) | copy-start | bytes 1769476
  87.6 2.2 %copy-start.8 = (bf16[64,4608]{1,0:T(8,128)(2,1)S(1)}, bf16[64,4608]{1,0:T(8,128)(2,1)}, u32[]{:S(2)}) copy-start(bf16[64,4608]{1,0:T(8,128)(2,1)} %copy-done.7) | copy-start | bytes 1769476
  93.1 2.5 %copy-start.27 = (bf16[1,384,4096]{2,1,0:T(8,128)(2,1)S(1)}, bf16[1,384,4096]{2,1,0:T(8,128)(2,1)}, u32[]{:S(2)}) copy-start(bf16[1,384,4096]{2,1,0:T(8,128)(2,1)} %param.13) | copy-start | bytes 9437188
  95.0 1.1 copy-start.15
  95.0 1.3 copy-start.19
  95.0 1.4 copy-start.21
  96.3 1.5 copy-start.3
  97.8 1.5 copy-start.23
  97.8 1.5 copy-start.17
  97.8 2.1 %copy-start.10 = (bf16[1,4096,384]{2,1,0:T(8,128)(2,1)S(1)}, bf16[1,4096,384]{2,1,0:T(8,128)(2,1)}, u32[]{:S(2)}) copy-start(bf16[1,4096,384]{2,1,0:T(8,128)(2,1)} %param.12) | copy-start | bytes 9437188
  101.3 1.5 copy-start.2
  105.4 13.3 %copy-start.1 = (bf16[256,4096]{1,0:T(8,128)(2,1)S(1)}, bf16[256,4096]{1,0:T(8,128)(2,1)}, u32[]{:S(2)}) copy-start(bf16[256,4096]{1,0:T(8,128)(2,1)} %slice.152) | copy-start | bytes 6291460
  106.6 12.1 %collective-permute-start.10 = (bf16[128,2304]{1,0:T(8,128)(2,1)S(1)}, bf16[128,2304]{1,0:T(8,128)(2,1)S(1)}, u32[]{:S(2)}, u32[]{:S(2)}) collective-permute-start(bf16[128,2304]{1,0:T(8,128)(2,1)S(1)} %pad_maximum_fusion.4), channel_id=1, source_target_pairs={{0,16},{8,24},{16,0},{24,8},{1,17},{9,25},{17,1},{25,9},{2,18},{10... | collective-permute-start | bytes 1769480 | tf_op jit(solution)/shard_map/ppermute | solution.py:43
  108.4 14.6 %collective-permute-start.8 = (bf16[128,2304]{1,0:T(8,128)(2,1)S(1)}, bf16[128,2304]{1,0:T(8,128)(2,1)S(1)}, u32[]{:S(2)}, u32[]{:S(2)}) collective-permute-start(bf16[128,2304]{1,0:T(8,128)(2,1)S(1)} %pad_maximum_fusion.7), channel_id=1, source_target_pairs={{0,8},{8,0},{16,24},{24,16},{1,9},{9,1},{17,25},{25,17},{2,10},{10... | collective-permute-start | bytes 1769480 | tf_op jit(solution)/shard_map/ppermute | solution.py:43
  118.8 7.7 %collective-permute-start.11 = (bf16[64,2304]{1,0:T(8,128)(2,1)S(1)}, bf16[64,2304]{1,0:T(8,128)(2,1)S(1)}, u32[]{:S(2)}, u32[]{:S(2)}) collective-permute-start(bf16[64,2304]{1,0:T(8,128)(2,1)S(1)} %add_convert_fusion.1), channel_id=1, source_target_pairs={{0,8},{8,0},{16,24},{24,16},{1,9},{9,1},{17,25},{25,17},{2,10},{10... | collective-permute-start | bytes 884744 | tf_op jit(solution)/shard_map/ppermute | solution.py:43
  124.0 6.8 %collective-permute-start.9 = (bf16[64,2304]{1,0:T(8,128)(2,1)S(1)}, bf16[64,2304]{1,0:T(8,128)(2,1)S(1)}, u32[]{:S(2)}, u32[]{:S(2)}) collective-permute-start(bf16[64,2304]{1,0:T(8,128)(2,1)S(1)} %add_convert_fusion.3), channel_id=1, source_target_pairs={{0,16},{8,24},{16,0},{24,8},{1,17},{9,25},{17,1},{25,9},{2,18},{10... | collective-permute-start | bytes 884744 | tf_op jit(solution)/shard_map/ppermute | solution.py:43
  126.6 10.5 %copy-start.24 = (bf16[288,384]{1,0:T(8,128)(2,1)S(1)}, bf16[288,384]{1,0:T(8,128)(2,1)}, u32[]{:S(2)}) copy-start(bf16[288,384]{1,0:T(8,128)(2,1)} %copy-done.23) | copy-start | bytes 663556
  132.7 21.0 %all-to-all-start.2 = ((bf16[8,8,4608]{2,1,0:T(8,128)(2,1)}), bf16[8,8,4608]{2,1,0:T(8,128)(2,1)}, u32[]{:S(2)}, u32[]{:S(2)}) async-start(bf16[8,8,4608]{2,1,0:T(8,128)(2,1)} %pad_maximum_fusion.8), calls=%async_computation.2 | async-start | bytes 1179648 | tf_op jit(solution)/shard_map/all_to_all | solution.py:74
  137.1 5.7 %copy-start.12 = (bf16[256,4096]{1,0:T(8,128)(2,1)S(1)}, bf16[256,4096]{1,0:T(8,128)(2,1)}, u32[]{:S(2)}) copy-start(bf16[256,4096]{1,0:T(8,128)(2,1)} %copy-done.11) | copy-start | bytes 6291460
  137.1 5.6 %copy-start.18 = (bf16[288,384]{1,0:T(8,128)(2,1)S(1)}, bf16[288,384]{1,0:T(8,128)(2,1)}, u32[]{:S(2)}) copy-start(bf16[288,384]{1,0:T(8,128)(2,1)} %copy-done.17) | copy-start | bytes 663556
  137.1 5.6 %copy-start.26 = (bf16[32,4096]{1,0:T(8,128)(2,1)S(1)}, bf16[32,4096]{1,0:T(8,128)(2,1)}, u32[]{:S(2)}) copy-start(bf16[32,4096]{1,0:T(8,128)(2,1)} %reshape.79) | copy-start | bytes 786436
  142.7 3.8 %copy-start.4 = (bf16[256,4096]{1,0:T(8,128)(2,1)S(1)}, bf16[256,4096]{1,0:T(8,128)(2,1)}, u32[]{:S(2)}) copy-start(bf16[256,4096]{1,0:T(8,128)(2,1)} %copy-done.3) | copy-start | bytes 6291460
  142.7 3.8 %copy-start.16 = (bf16[32,4096]{1,0:T(8,128)(2,1)S(1)}, bf16[32,4096]{1,0:T(8,128)(2,1)}, u32[]{:S(2)}) copy-start(bf16[32,4096]{1,0:T(8,128)(2,1)} %reshape.77) | copy-start | bytes 786436
  142.8 3.8 %copy-start.20 = (f32[288,384]{1,0:T(8,128)S(1)}, f32[288,384]{1,0:T(8,128)}, u32[]{:S(2)}) copy-start(f32[288,384]{1,0:T(8,128)} %fusion.6) | copy-start | bytes 1327108
  142.8 3.8 %copy-start.22 = (f32[288,384]{1,0:T(8,128)S(1)}, f32[288,384]{1,0:T(8,128)}, u32[]{:S(2)}) copy-start(f32[288,384]{1,0:T(8,128)} %fusion.9) | copy-start | bytes 1327108

commit v2 on v1

--- a/solution.py
+++ b/solution.py
@@ -1,6 +1,10 @@
+import functools
+
 import jax
 import jax.numpy as jnp
 from jax import lax
+from jax.experimental import pallas as pl
+from jax.experimental.pallas import tpu as pltpu
 from jax.sharding import PartitionSpec as P
 
 CAP = 9
@@ -43,13 +47,141 @@
     return lax.ppermute(value, "dp", [(i, i ^ bit) for i in range(DP)])
 
 
-def gather(own):
-    half = own.shape[1] // 2
-    one = swap(own, 1)
-    two = swap(own, 2)
-    three_a = swap(one[:, :half], 2)
-    three_b = swap(two[:, half:], 1)
-    return jnp.concatenate([own, one, two, jnp.concatenate([three_a, three_b], axis=1)], axis=0)
+def visit_order(experts):
+    order = [0]
+    for k in range(1, experts // 2 + 1):
+        order.append(k)
+        if experts - k != k:
+            order.append(experts - k)
+    return order
+
+
+def enter(me, pe, experts, neighbours):
+    barrier = pltpu.get_barrier_semaphore()
+    for k in range(1, experts):
+        pl.semaphore_signal(
+            barrier,
+            inc=1,
+            device_id=(me, lax.rem(pe + k, experts)),
+            device_id_type=pl.DeviceIdType.MESH,
+        )
+    for other in neighbours:
+        pl.semaphore_signal(
+            barrier, inc=1, device_id=(other, pe), device_id_type=pl.DeviceIdType.MESH
+        )
+    pl.semaphore_wait(barrier, experts - 1 + len(neighbours))
+
+
+def remote(src, dst, sems, slot, device):
+    return pltpu.make_async_remote_copy(
+        src_ref=src,
+        dst_ref=dst,
+        send_sem=sems.at[0, slot],
+        recv_sem=sems.at[1, slot],
+        device_id=device,
+        device_id_type=pl.DeviceIdType.MESH,
+    )
+
+
+def dispatch_kernel(experts, send, got, own_sem, z_sem, x_sem, y_sem, xy_sem, yx_sem):
+    me, pe = lax.axis_index("dp"), lax.axis_index("expert")
+    along_x = me + 1 - 2 * lax.rem(me, 2)
+    along_y = lax.rem(me + 2, DP)
+    half = send.shape[2] // 2
+    first, last = pl.ds(0, half), pl.ds(half, half)
+    enter(me, pe, experts, (along_x, along_y))
+    own = pltpu.make_async_copy(send.at[pe], got.at[0, pe], own_sem)
+    own.start()
+    order = visit_order(experts)
+    across = {}
+    for k in order[1:]:
+        to = lax.rem(pe + k, experts)
+        across[k] = remote(send.at[to], got.at[0, pe], z_sem, k, (me, to))
+        across[k].start()
+    copies = {}
+    for step in range(experts + 1):
+        if step < experts:
+            k = order[step]
+            block = lax.rem(pe + experts - k, experts)
+            if k == 0:
+                source = send.at[pe]
+            else:
+                across[k].wait_recv()
+                source = got.at[0, block]
+            ways = (
+                remote(source, got.at[1, block], x_sem, k, (along_x, pe)),
+                remote(source, got.at[2, block], y_sem, k, (along_y, pe)),
+            )
+            for way in ways:
+                way.start()
+            copies[k] = list(ways)
+        if step >= 1:
+            k = order[step - 1]
+            block = lax.rem(pe + experts - k, experts)
+            copies[k][0].wait_recv()
+            onward = remote(
+                got.at[1, block, :, first], got.at[3, block, :, first], xy_sem, k, (along_y, pe)
+            )
+            onward.start()
+            copies[k].append(onward)
+            copies[k][1].wait_recv()
+            onward = remote(
+                got.at[2, block, :, last], got.at[3, block, :, last], yx_sem, k, (along_x, pe)
+            )
+            onward.start()
+            copies[k].append(onward)
+    own.wait()
+    for k in order:
+        if k != 0:
+            across[k].wait_send()
+        for copy in copies[k]:
+            copy.wait_send()
+        copies[k][2].wait_recv()
+        copies[k][3].wait_recv()
+
+
+def dispatch(send):
+    experts = send.shape[0]
+    pairs = pltpu.SemaphoreType.DMA((2, experts))
+    size = send.size * send.dtype.itemsize
+    return pl.pallas_call(
+        functools.partial(dispatch_kernel, experts),
+        out_shape=jax.ShapeDtypeStruct((DP,) + send.shape, send.dtype),
+        in_specs=[pl.BlockSpec(memory_space=pl.ANY)],
+        out_specs=pl.BlockSpec(memory_space=pl.ANY),
+        scratch_shapes=[pltpu.SemaphoreType.DMA(())] + [pairs] * 5,
+        compiler_params=pltpu.CompilerParams(collective_id=0, has_side_effects=True),
+        cost_estimate=pl.CostEstimate(flops=0, bytes_accessed=8 * size, transcendentals=0),
+    )(send)
+
+
+def exchange_kernel(experts, send, got, own_sem, z_sem):
+    me, pe = lax.axis_index("dp"), lax.axis_index("expert")
+    enter(me, pe, experts, ())
+    own = pltpu.make_async_copy(send.at[pe], got.at[pe], own_sem)
+    own.start()
+    across = []
+    for k in visit_order(experts)[1:]:
+        to = lax.rem(pe + k, experts)
+        across.append(remote(send.at[to], got.at[pe], z_sem, k, (me, to)))
+        across[-1].start()
+    own.wait()
+    for copy in across:
+        copy.wait()
+
+
+def exchange(send):
+    experts = send.shape[0]
+    size = send.size * send.dtype.itemsize
+    return pl.pallas_call(
+        functools.partial(exchange_kernel, experts),
+        out_shape=jax.ShapeDtypeStruct(send.shape, send.dtype),
+        in_specs=[pl.BlockSpec(memory_space=pl.ANY)],
+        out_specs=pl.BlockSpec(memory_space=pl.ANY),
+        scratch_shapes=[pltpu.SemaphoreType.DMA(()), pltpu.SemaphoreType.DMA((2, experts))],
+        compiler_params=pltpu.CompilerParams(collective_id=1, has_side_effects=True),
+        cost_estimate=pl.CostEstimate(flops=0, bytes_accessed=4 * size, transcendentals=0),
+    )(send)
 
 
 def reduce_to_own(parts):
@@ -67,12 +199,6 @@
     a = way(slice(0, half), 1, 2)
     b = way(slice(half, 2 * half), 2, 1)
     return jnp.concatenate([a, b], axis=1).astype(jnp.bfloat16)
-
-
-def exchange(packed, experts):
-    blocks = packed.reshape(experts, MAIN, -1)
-    got = lax.all_to_all(blocks, "expert", split_axis=0, concat_axis=0, tiled=True)
-    return got.reshape(packed.shape)
 
 
 def shards(tokens, out_grad, expert_ids, gate_weights, w_gate, w_up, w_down):
@@ -83,8 +209,10 @@
     place_bf = place.astype(bf16)
     send_x = jnp.dot(place_bf, tokens, preferred_element_type=f32).astype(bf16)
     send_dy = jnp.dot(scaled, out_grad.astype(f32), precision=lax.Precision.HIGHEST).astype(bf16)
-    slot_x = unpack(gather(exchange(pack(send_x), experts)), width)
-    slot_dy = unpack(gather(exchange(pack(send_dy), experts)), width)
+    both = [pack(rows).reshape(experts, MAIN, -1) for rows in (send_x, send_dy)]
+    got = dispatch(jnp.concatenate(both, axis=1))
+    slot_x = unpack(got[:, :, :MAIN].reshape(DP * experts * MAIN, -1), width)
+    slot_dy = unpack(got[:, :, MAIN:].reshape(DP * experts * MAIN, -1), width)
     wg = w_gate[0]
     wu = w_up[0]
     wd = w_down[0]
@@ -101,7 +229,14 @@
     gate_grad = lax.dot_general(slot_x, d_gate, OVER_ROWS, preferred_element_type=f32).astype(bf16)
     up_grad = lax.dot_general(slot_x, d_up, OVER_ROWS, preferred_element_type=f32).astype(bf16)
     down_grad = lax.dot_general(act, slot_dy, OVER_ROWS, preferred_element_type=f32).astype(bf16)
-    returned = unpack(exchange(slot_grad, experts), width)
+    slot_grad, gate_grad, up_grad, down_grad = lax.optimization_barrier(
+        (slot_grad, gate_grad, up_grad, down_grad)
+    )
+    blocks = slot_grad.reshape(experts, MAIN, -1)
+    half = blocks.shape[2] // 2
+    back = exchange(jnp.concatenate([blocks[:, :, :half], blocks[:, :, half:]], axis=1))
+    back = jnp.concatenate([back[:, :MAIN], back[:, MAIN:]], axis=2)
+    returned = unpack(back.reshape(experts * MAIN, -1), width)
     token_grad = lax.dot_general(place_bf, returned, OVER_ROWS, preferred_element_type=f32)
     return (token_grad.astype(bf16), gate_grad[None], up_grad[None], down_grad[None])
 

time: 160 us -> 134 us (0.84)
  Pallas kernels: 0 us -> 63.8 us
  waiting for transfers between devices: 59.4 us -> 10.1 us
  starting transfers between devices: 30.8 us -> 4.12 us
  other arithmetic: 17 us -> 7.89 us
  local copies, waits for them, and re-layouts: 23.2 us -> 17.2 us
  matrix products: 27.4 us -> 29.2 us
    pallas_call x0 -> x2, Pallas kernels: none -> 63.8 us  [the longest x1 46.7 us: dispatch(): pl.pallas_call(functools.partial(dispatch_kernel, experts), out_shape=jax...]
    all_to_all x3 -> x0, waiting for transfers between devices: 31.3 us -> none  [exchange(): lax.all_to_all(blocks, 'expert', split_axis=0, concat_axis=0, tiled=True)]
    ppermute x12 -> x4, waiting for transfers between devices: 28.1 us -> 10.1 us  [swap(): return lax.ppermute(value, 'dp', [(i, i ^ bit) for i in range(DP)])]
    all_to_all x3 -> x0, starting transfers between devices: 14.9 us -> none  [exchange(): lax.all_to_all(blocks, 'expert', split_axis=0, concat_axis=0, tiled=True)]
    ppermute x12 -> x4, starting transfers between devices: 15.9 us -> 4.12 us  [swap(): return lax.ppermute(value, 'dp', [(i, i ^ bit) for i in range(DP)])]
    unnamed x57 -> x41, local copies, waits for them, and re-layouts: 7.71 us -> 2.35 us
    concatenate x4 -> x2, other arithmetic: 5.27 us -> 1.96 us  [the longest x1 1.1 us: shards(): got = dispatch(jnp.concatenate(both, axis=1))]
    slice x2 -> x0, other arithmetic: 3.18 us -> none  [unpack(): extra = packed[:, width:].reshape(packed.shape[0] // MAIN, width)]
  transfers between devices with their start and end apart: 15 -> 4, of which waited for: 9 -> 4; matrix products, arithmetic and copies ran while one was open for 20% -> 9% of each run, Pallas kernels for 0% -> 0%
where the time goes in v2:
time: 134 us; the launch traced here: 133 us
  Pallas kernels  63.8 us (48%)
  matrix products  29.2 us (22%)
  local copies, waits for them, and re-layouts  17.2 us (13%)
  waiting for transfers between devices  10.1 us (8%)
  other arithmetic  7.89 us (6%)
  starting transfers between devices  4.12 us (3%)
    pallas_call x1, Pallas kernels, dispatch(): pl.pallas_call(functools.partial(dispatch_kernel, experts), out_shape=jax...  46.7 us
    pallas_call x1, Pallas kernels, exchange(): pl.pallas_call(functools.partial(exchange_kernel, experts), out_shape=jax...  17 us
    ppermute x4, waiting for transfers between devices, swap(): return lax.ppermute(value, 'dp', [(i, i ^ bit) for i in range(DP)])  10.1 us
    dot_general x1, matrix products, shards(): d_act = lax.dot_general(slot_dy, wd, OVER_UNITS, preferred_element_type=f32)  4.26 us
    ppermute x4, starting transfers between devices, swap(): return lax.ppermute(value, 'dp', [(i, i ^ bit) for i in range(DP)])  4.12 us
    slice x3, local copies, waits for them, and re-layouts, unpack(): main = packed[:, :width]  4.04 us
    dot_general x1, matrix products, shards(): lax.dot_general(slot_x, d_up, OVER_ROWS, preferred_element_type=f32)  4 us
    dot_general x1, matrix products, shards(): gate = jnp.dot(slot_x, wg, preferred_element_type=f32)  3.96 us
  transfers between devices with their start and end apart: 4, of which 4 were waited for; matrix products, arithmetic and copies ran while one was open for 9% of the time, Pallas kernels for 0%

profile of v2, /device:TPU:0, one launch (start us, length us, event | category | flops | bytes accessed | tf_op | source)
XLA Modules:
  0.0 133.3 jit_solution(2093637798507122736)
XLA Ops:
  0.6 0.0 copy-start
  0.6 0.9 copy.33
  1.6 0.1 eq.43
  1.7 0.1 eq.39
  1.8 2.3 %reduce-window.6 = s32[8,8,128]{2,1,0:T(8,128)S(1)} reduce-window(s32[8,8,128]{2,1,0:T(8,128)S(1)} %fusion.17, s32[]{:T(128)} %constant.3.clone.1), window={size=1x1x128 pad=0_0x0_0x127_0}, to_apply=%region_0.0 | reduce-window | flops 1040384 | bytes 65540 | tf_op jit(solution)/shard_map/reduce-window
  4.1 0.3 slice_reduce_fusion
  4.3 0.2 reduce-window.9
  4.5 0.1 add_bitcast_fusion
  4.6 0.1 reduce_sum.30
  4.7 0.8 select_select_fusion
  5.6 0.9 convert_reduce_fusion
  6.4 1.8 %convolution_convert_fusion.5 = bf16[72,4096]{1,0:T(8,128)(2,1)S(1)} fusion(f32[72,128]{1,0:T(8,128)S(1)} %get-tuple-element.13, bf16[128,4096]{1,0:T(8,128)(2,1)} %param.8), kind=kOutput, calls=%fused_computation.7 | convolution fusion | flops 453279744 | bytes 1675264 | tf_op jit(solution)/shard_map/dot_general | solution.py:211
  8.3 0.0 copy-done.9
  8.3 0.3 convolution_convert_fusion.4
  8.6 0.1 slice_bitcast_fusion
  8.8 1.1 maximum_maximum_fusion.send
  9.9 46.7 %shard_map.102 = bf16[4,8,16,4608]{3,2,1,0:T(8,128)(2,1)} custom-call(bf16[8,16,4608]{2,1,0:T(8,128)(2,1)} %maximum_maximum_fusion.send), custom_call_target="tpu_custom_call" | custom-call | bytes 9437184 | tf_op jit(solution)/shard_map/pallas_call | solution.py:147
  56.6 2.8 %fusion.24 = (bf16[4,8,8,4608]{3,2,1,0:T(8,128)(2,1)S(1)}, bf16[4,8,8,4608]{3,2,1,0:T(8,128)(2,1)S(1)}) fusion(bf16[4,8,16,4608]{3,2,1,0:T(8,128)(2,1)} %shard_map.102), kind=kLoop, calls=%fused_computation.61 | loop fusion | bytes 9437184 | tf_op jit(solution)/shard_map/slice | solution.py:215
  59.5 1.6 %slice.150 = bf16[256,4096]{1,0:T(8,128)(2,1)} slice(bf16[256,4608]{1,0:T(8,128)(2,1)S(1)} %bitcast.64), slice={[0:256], [0:4096]} | slice | bytes 4194304 | tf_op jit(solution)/shard_map/slice | solution.py:41
  61.1 0.7 slice.149
  61.8 1.6 %slice.148 = bf16[256,4096]{1,0:T(8,128)(2,1)} slice(bf16[256,4608]{1,0:T(8,128)(2,1)S(1)} %bitcast.62), slice={[0:256], [0:4096]} | slice | bytes 4194304 | tf_op jit(solution)/shard_map/slice | solution.py:41
  63.4 0.8 reshape.77
  64.3 0.0 copy-done
  64.3 4.0 %fusion.3 = f32[288,384]{1,0:T(8,128)} fusion(bf16[1,4096,384]{2,1,0:T(8,128)(2,1)S(1)} %copy-done, bf16[32,4096]{1,0:T(8,128)(2,1)} %reshape.77, bf16[256,4096]{1,0:T(8,128)(2,1)} %slice.150), kind=kOutput, calls=%fused_computation.10 | convolution fusion | flops 910688256 | bytes 5947392 | tf_op jit(solution)/shard_map/dot_general | solution.py:219
  68.3 2.2 %fusion.6 = f32[288,384]{1,0:T(8,128)} fusion(bf16[1,4096,384]{2,1,0:T(8,128)(2,1)S(1)} %copy-done.5, bf16[32,4096]{1,0:T(8,128)(2,1)S(1)} %copy-done.18, bf16[256,4096]{1,0:T(8,128)(2,1)S(1)} %copy-done.7), kind=kOutput, calls=%fused_computation.13 | convolution fusion | flops 910688256 | bytes 5947392 | tf_op jit(solution)/shard_map/dot_general | solution.py:220
  70.4 1.1 reshape.75
  71.5 4.3 %multiply_convert_fusion.1 = (bf16[288,384]{1,0:T(8,128)(2,1)S(1)}, bf16[288,384]{1,0:T(8,128)(2,1)S(1)}) fusion(f32[288,384]{1,0:T(8,128)} %fusion.3, f32[288,384]{1,0:T(8,128)} %fusion.6, bf16[1,384,4096]{2,1,0:T(8,128)(2,1)} %param.13, bf16[32,4096]{1,0:T(8,128)(2,1)S(1)} %reshape.75, bf16[256,4096]{1,0:T(8,128)(2,1)} %slice.148), kind=kOutput, calls=%fused_computation.35 | convolution fusion | flops 912125952 | bytes 6832128 | tf_op jit(solution)/shard_map/dot_general | solution.py:223
  75.8 0.0 copy-start.6
  75.8 1.4 %fusion.1 = f32[288,4096]{1,0:T(8,128)S(1)} fusion(bf16[288,384]{1,0:T(8,128)(2,1)S(1)} %get-tuple-element.19, bf16[1,4096,384]{2,1,0:T(8,128)(2,1)S(1)} %copy-done), kind=kOutput, calls=%fused_computation.8 | convolution fusion | flops 905969664 | bytes 8085504 | tf_op jit(solution)/shard_map/dot_general | solution.py:226
  77.3 0.6 copy-done.6
  77.9 1.4 %fusion = bf16[288,4096]{1,0:T(8,128)(2,1)S(1)} fusion(f32[288,4096]{1,0:T(8,128)S(1)} %fusion.1, bf16[288,384]{1,0:T(8,128)(2,1)S(1)} %get-tuple-element.18, bf16[1,4096,384]{2,1,0:T(8,128)(2,1)S(1)} %copy-done.6), kind=kOutput, calls=%fused_computation.4 | convolution fusion | flops 908328960 | bytes 10444800 | tf_op jit(solution)/shard_map/dot_general | solution.py:227
  79.3 0.0 copy-start.2
  79.3 0.7 slice.159
  80.0 0.7 copy-done.2
  80.8 1.5 %slice.158 = bf16[256,4096]{1,0:T(8,128)(2,1)} slice(bf16[288,4096]{1,0:T(8,128)(2,1)S(1)} %fusion), slice={[0:256], [0:4096]} | slice | bytes 4194304 | tf_op jit(solution)/shard_map/slice | solution.py:35
  82.3 1.1 reshape.78
  83.4 0.0 copy-start.3
  83.4 0.0 copy-start.8
  83.4 0.0 copy-start.19
  83.4 1.2 pad_maximum_fusion.4
  84.6 0.7 collective-permute-start.2
  85.4 0.0 copy-start.13
  85.4 1.5 %collective-permute-start = (bf16[128,2304]{1,0:T(8,128)(2,1)S(1)}, bf16[128,2304]{1,0:T(8,128)(2,1)S(1)}, u32[]{:S(2)}, u32[]{:S(2)}) collective-permute-start(bf16[128,2304]{1,0:T(8,128)(2,1)S(1)} %pad_maximum_fusion.5), channel_id=1, source_target_pairs={{0,8},{8,0},{16,24},{24,16},{1,9},{9,1},{17,25},{25,17},{2,10},{10... | collective-permute-start | bytes 1769480 | tf_op jit(solution)/shard_map/ppermute | solution.py:47
  86.9 3.8 %convolution_convert_fusion.2 = bf16[4096,384]{1,0:T(8,128)(2,1)} fusion(bf16[288,384]{1,0:T(8,128)(2,1)S(1)} %copy-done.17, bf16[32,4096]{1,0:T(8,128)(2,1)S(1)} %copy-done.19, bf16[256,4096]{1,0:T(8,128)(2,1)S(1)} %copy-done.8), kind=kOutput, calls=%fused_computation.3 | convolution fusion | flops 912261120 | bytes 5726208 | tf_op jit(solution)/shard_map/dot_general | solution.py:229
  90.7 4.0 %convolution_convert_fusion.1 = bf16[4096,384]{1,0:T(8,128)(2,1)} fusion(bf16[288,384]{1,0:T(8,128)(2,1)S(1)} %copy-done.13, bf16[32,4096]{1,0:T(8,128)(2,1)S(1)} %copy-done.19, bf16[256,4096]{1,0:T(8,128)(2,1)S(1)} %copy-done.8), kind=kOutput, calls=%fused_computation.2 | convolution fusion | flops 912261120 | bytes 5726208 | tf_op jit(solution)/shard_map/dot_general | solution.py:230
  94.7 0.0 copy-done.11
  94.7 0.0 copy-done.15
  94.7 3.5 %convolution_convert_fusion = bf16[384,4096]{1,0:T(8,128)(2,1)} fusion(bf16[32,4096]{1,0:T(8,128)(2,1)S(1)} %copy-done.11, bf16[256,4096]{1,0:T(8,128)(2,1)S(1)} %copy-done.4, f32[288,384]{1,0:T(8,128)S(1)} %copy-done.15, f32[288,384]{1,0:T(8,128)S(1)} %copy-done.14), kind=kOutput, calls=%fused_computation.1 | convolution fusion | flops 912924672 | bytes 6389760 | tf_op jit(solution)/shard_map/dot_general | solution.py:231
  98.3 2.3 %collective-permute-done.2 = bf16[128,2304]{1,0:T(8,128)(2,1)S(1)} collective-permute-done((bf16[128,2304]{1,0:T(8,128)(2,1)S(1)}, bf16[128,2304]{1,0:T(8,128)(2,1)S(1)}, u32[]{:S(2)}, u32[]{:S(2)}) %collective-permute-start.2) | collective-permute-done | bytes 589856 | tf_op jit(solution)/shard_map/ppermute | solution.py:47
  100.6 0.0 copy-done.1
  100.6 0.1 add_convert_fusion.1
  100.7 0.7 collective-permute-start.3
  101.4 0.2 collective-permute-done
  101.5 0.1 add_convert_fusion.3
  101.6 1.3 collective-permute-start.1
  102.9 6.5 %collective-permute-done.3 = bf16[64,2304]{1,0:T(8,128)(2,1)S(1)} collective-permute-done((bf16[64,2304]{1,0:T(8,128)(2,1)S(1)}, bf16[64,2304]{1,0:T(8,128)(2,1)S(1)}, u32[]{:S(2)}, u32[]{:S(2)}) %collective-permute-start.3) | collective-permute-done | bytes 294944 | tf_op jit(solution)/shard_map/ppermute | solution.py:47
  109.4 0.1 add_convert_fusion
  109.6 1.1 collective-permute-done.1
  110.7 0.1 add_convert_fusion.2
  110.9 0.9 pad_maximum_fusion.7.send
  111.8 17.0 %shard_map.103 = bf16[8,16,2304]{2,1,0:T(8,128)(2,1)} custom-call(bf16[8,16,2304]{2,1,0:T(8,128)(2,1)} %pad_maximum_fusion.7.send), custom_call_target="tpu_custom_call" | custom-call | bytes 2359296 | tf_op jit(solution)/shard_map/pallas_call | solution.py:176
  128.8 1.1 fusion.26
  130.0 0.8 slice.164
  130.8 2.5 %convolution_convert_fusion.3 = bf16[128,4096]{1,0:T(8,128)(2,1)} fusion(bf16[8,4096]{1,0:T(8,128)(2,1)S(1)} %reshape.81, bf16[64,4096]{1,0:T(8,128)(2,1)} %slice.164, bf16[72,128]{1,0:T(8,128)(2,1)S(1)} %get-tuple-element.12), kind=kOutput, calls=%fused_computation.5 | convolution fusion | flops 77201408 | bytes 1656832 | tf_op jit(solution)/shard_map/dot_general | solution.py:240
  (40 shorter events, 0.5 us)
Async XLA Ops:
  0.6 63.6 %copy-start = (bf16[1,4096,384]{2,1,0:T(8,128)(2,1)S(1)}, bf16[1,4096,384]{2,1,0:T(8,128)(2,1)}, u32[]{:S(2)}) copy-start(bf16[1,4096,384]{2,1,0:T(8,128)(2,1)} %param.11) | copy-start | bytes 9437188
  4.7 3.5 %copy-start.9 = (bf16[128,4096]{1,0:T(8,128)(2,1)S(1)}, bf16[128,4096]{1,0:T(8,128)(2,1)}, u32[]{:S(2)}) copy-start(bf16[128,4096]{1,0:T(8,128)(2,1)} %param.7) | copy-start | bytes 3145732
  64.3 4.0 %copy-start.5 = (bf16[1,4096,384]{2,1,0:T(8,128)(2,1)S(1)}, bf16[1,4096,384]{2,1,0:T(8,128)(2,1)}, u32[]{:S(2)}) copy-start(bf16[1,4096,384]{2,1,0:T(8,128)(2,1)} %param.12) | copy-start | bytes 9437188
  64.3 4.0 %copy-start.7 = (bf16[256,4096]{1,0:T(8,128)(2,1)S(1)}, bf16[256,4096]{1,0:T(8,128)(2,1)}, u32[]{:S(2)}) copy-start(bf16[256,4096]{1,0:T(8,128)(2,1)} %slice.150) | copy-start | bytes 6291460
  64.3 4.0 %copy-start.18 = (bf16[32,4096]{1,0:T(8,128)(2,1)S(1)}, bf16[32,4096]{1,0:T(8,128)(2,1)}, u32[]{:S(2)}) copy-start(bf16[32,4096]{1,0:T(8,128)(2,1)} %reshape.77) | copy-start | bytes 786436
  71.5 4.3 %copy-start.10 = (bf16[32,4096]{1,0:T(8,128)(2,1)}, bf16[32,4096]{1,0:T(8,128)(2,1)S(1)}, u32[]{:S(2)}) copy-start(bf16[32,4096]{1,0:T(8,128)(2,1)S(1)} %reshape.75) | copy-start | bytes 786436
  75.8 1.5 %copy-start.16 = (bf16[288,384]{1,0:T(8,128)(2,1)}, bf16[288,384]{1,0:T(8,128)(2,1)S(1)}, u32[]{:S(2)}) copy-start(bf16[288,384]{1,0:T(8,128)(2,1)S(1)} %get-tuple-element.19) | copy-start | bytes 663556
  75.8 1.5 %copy-start.12 = (bf16[288,384]{1,0:T(8,128)(2,1)}, bf16[288,384]{1,0:T(8,128)(2,1)S(1)}, u32[]{:S(2)}) copy-start(bf16[288,384]{1,0:T(8,128)(2,1)S(1)} %get-tuple-element.18) | copy-start | bytes 663556
  75.8 2.1 %copy-start.6 = (bf16[1,4096,384]{2,1,0:T(8,128)(2,1)S(1)}, bf16[1,4096,384]{2,1,0:T(8,128)(2,1)}, u32[]{:S(2)}) copy-start(bf16[1,4096,384]{2,1,0:T(8,128)(2,1)} %param.12) | copy-start | bytes 9437188
  79.3 1.5 %copy-start.2 = (bf16[288,4096]{1,0:T(8,128)(2,1)}, bf16[288,4096]{1,0:T(8,128)(2,1)S(1)}, u32[]{:S(2)}) copy-start(bf16[288,4096]{1,0:T(8,128)(2,1)S(1)} %fusion) | copy-start | bytes 7077892
  83.4 1.9 %copy-start.3 = (bf16[288,4096]{1,0:T(8,128)(2,1)S(1)}, bf16[288,4096]{1,0:T(8,128)(2,1)}, u32[]{:S(2)}) copy-start(bf16[288,4096]{1,0:T(8,128)(2,1)} %copy-done.2) | copy-start | bytes 7077892
  83.4 3.5 %copy-start.8 = (bf16[256,4096]{1,0:T(8,128)(2,1)S(1)}, bf16[256,4096]{1,0:T(8,128)(2,1)}, u32[]{:S(2)}) copy-start(bf16[256,4096]{1,0:T(8,128)(2,1)} %slice.150) | copy-start | bytes 6291460
  83.4 3.5 %copy-start.17 = (bf16[288,384]{1,0:T(8,128)(2,1)S(1)}, bf16[288,384]{1,0:T(8,128)(2,1)}, u32[]{:S(2)}) copy-start(bf16[288,384]{1,0:T(8,128)(2,1)} %copy-done.16) | copy-start | bytes 663556
  83.4 3.5 %copy-start.19 = (bf16[32,4096]{1,0:T(8,128)(2,1)S(1)}, bf16[32,4096]{1,0:T(8,128)(2,1)}, u32[]{:S(2)}) copy-start(bf16[32,4096]{1,0:T(8,128)(2,1)} %reshape.77) | copy-start | bytes 786436
  84.6 15.9 %collective-permute-start.2 = (bf16[128,2304]{1,0:T(8,128)(2,1)S(1)}, bf16[128,2304]{1,0:T(8,128)(2,1)S(1)}, u32[]{:S(2)}, u32[]{:S(2)}) collective-permute-start(bf16[128,2304]{1,0:T(8,128)(2,1)S(1)} %pad_maximum_fusion.4), channel_id=1, source_target_pairs={{0,16},{8,24},{16,0},{24,8},{1,17},{9,25},{17,1},{25,9},{2,18},{10... | collective-permute-start | bytes 1769480 | tf_op jit(solution)/shard_map/ppermute | solution.py:47
  85.4 5.3 %copy-start.13 = (bf16[288,384]{1,0:T(8,128)(2,1)S(1)}, bf16[288,384]{1,0:T(8,128)(2,1)}, u32[]{:S(2)}) copy-start(bf16[288,384]{1,0:T(8,128)(2,1)} %copy-done.12) | copy-start | bytes 663556
  85.4 16.1 %collective-permute-start = (bf16[128,2304]{1,0:T(8,128)(2,1)S(1)}, bf16[128,2304]{1,0:T(8,128)(2,1)S(1)}, u32[]{:S(2)}, u32[]{:S(2)}) collective-permute-start(bf16[128,2304]{1,0:T(8,128)(2,1)S(1)} %pad_maximum_fusion.5), channel_id=1, source_target_pairs={{0,8},{8,0},{16,24},{24,16},{1,9},{9,1},{17,25},{25,17},{2,10},{10... | collective-permute-start | bytes 1769480 | tf_op jit(solution)/shard_map/ppermute | solution.py:47
  90.7 4.0 %copy-start.4 = (bf16[256,4096]{1,0:T(8,128)(2,1)S(1)}, bf16[256,4096]{1,0:T(8,128)(2,1)}, u32[]{:S(2)}) copy-start(bf16[256,4096]{1,0:T(8,128)(2,1)} %slice.148) | copy-start | bytes 6291460
  90.7 4.0 %copy-start.11 = (bf16[32,4096]{1,0:T(8,128)(2,1)S(1)}, bf16[32,4096]{1,0:T(8,128)(2,1)}, u32[]{:S(2)}) copy-start(bf16[32,4096]{1,0:T(8,128)(2,1)} %copy-done.10) | copy-start | bytes 786436
  90.7 4.0 %copy-start.14 = (f32[288,384]{1,0:T(8,128)S(1)}, f32[288,384]{1,0:T(8,128)}, u32[]{:S(2)}) copy-start(f32[288,384]{1,0:T(8,128)} %fusion.3) | copy-start | bytes 1327108
  90.7 4.0 %copy-start.15 = (f32[288,384]{1,0:T(8,128)S(1)}, f32[288,384]{1,0:T(8,128)}, u32[]{:S(2)}) copy-start(f32[288,384]{1,0:T(8,128)} %fusion.6) | copy-start | bytes 1327108
  94.7 5.9 %copy-start.1 = (bf16[256,4096]{1,0:T(8,128)(2,1)S(1)}, bf16[256,4096]{1,0:T(8,128)(2,1)}, u32[]{:S(2)}) copy-start(bf16[256,4096]{1,0:T(8,128)(2,1)} %slice.158) | copy-start | bytes 6291460
  100.7 8.8 %collective-permute-start.3 = (bf16[64,2304]{1,0:T(8,128)(2,1)S(1)}, bf16[64,2304]{1,0:T(8,128)(2,1)S(1)}, u32[]{:S(2)}, u32[]{:S(2)}) collective-permute-start(bf16[64,2304]{1,0:T(8,128)(2,1)S(1)} %add_convert_fusion.1), channel_id=1, source_target_pairs={{0,8},{8,0},{16,24},{24,16},{1,9},{9,1},{17,25},{25,17},{2,10},{10... | collective-permute-start | bytes 884744 | tf_op jit(solution)/shard_map/ppermute | solution.py:47
  101.6 9.1 %collective-permute-start.1 = (bf16[64,2304]{1,0:T(8,128)(2,1)S(1)}, bf16[64,2304]{1,0:T(8,128)(2,1)S(1)}, u32[]{:S(2)}, u32[]{:S(2)}) collective-permute-start(bf16[64,2304]{1,0:T(8,128)(2,1)S(1)} %add_convert_fusion.3), channel_id=1, source_target_pairs={{0,16},{8,24},{16,0},{24,8},{1,17},{9,25},{17,1},{25,9},{2,18},{10... | collective-permute-start | bytes 884744 | tf_op jit(solution)/shard_map/ppermute | solution.py:47

commit v3 on v2

--- a/solution.py
+++ b/solution.py
@@ -27,6 +27,108 @@
     place = jnp.sum(hits.astype(jnp.float32), axis=2)
     scaled = jnp.sum(jnp.where(hits, gate_weights[None, :, :], jnp.float32(0.0)), axis=2)
     return (place, scaled)
+
+
+def one_hot(shape, column_of_row, dim=0):
+    along = lax.broadcasted_iota(jnp.int32, shape, dim)
+    across = lax.broadcasted_iota(jnp.int32, shape, 1 - dim)
+    return (column_of_row(along) == across).astype(jnp.bfloat16)
+
+
+def expert_kernel(
+    z, z_extra, wg, wu, wd, x, dy, act, d_gate, d_up, partial, gate_sum, up_sum, act_sum, extra_sum
+):
+    f32, bf16 = jnp.float32, jnp.bfloat16
+    step = pl.program_id(0)
+    rows2 = z.shape[0]
+    main = rows2 // 2
+    blocks = main // MAIN
+
+    def dot(a, b, dims=(((1,), (0,)), ((), ()))):
+        return lax.dot_general(a, b, dims, preferred_element_type=f32)
+
+    @pl.when(step == 0)
+    def _():
+        for total in (gate_sum, up_sum, act_sum):
+            total[...] = jnp.zeros_like(total)
+
+    @pl.when(step < MAIN)
+    def _():
+        for out, offset in ((x, 0), (dy, MAIN)):
+            pick = one_hot((main, rows2), lambda r: (r // MAIN) * 2 * MAIN + r % MAIN + offset)
+            out[:main, :] = dot(pick, z[...]).astype(bf16)
+            pick = one_hot((blocks, rows2), lambda r: r * 2 * MAIN + offset + step)
+            out[main:, :] = dot(pick, z_extra[...]).astype(bf16)
+        gate_sum[...] += dot(x[...], wg[...])
+        up_sum[...] += dot(x[...], wu[...])
+        act_sum[...] += dot(dy[...], wd[...], OVER_UNITS)
+
+    @pl.when(step == MAIN - 1)
+    def _():
+        gate, up, d_act = gate_sum[...], up_sum[...], act_sum[...]
+        sig = jax.nn.sigmoid(gate)
+        act[...] = (gate * sig * up).astype(bf16)
+        d_up[...] = (d_act * gate * sig).astype(bf16)
+        d_gate[...] = (d_act * up * sig * (1.0 + gate * (1.0 - sig))).astype(bf16)
+        extra_sum[...] = jnp.zeros_like(extra_sum)
+
+    @pl.when((step >= MAIN) & (step < 2 * MAIN))
+    def _():
+        value = dot(d_gate[...], wg[...], OVER_UNITS) + dot(d_up[...], wu[...], OVER_UNITS)
+        value = value.astype(bf16)
+        partial[...] = value[:main]
+        put = one_hot((main, blocks), lambda r: r * MAIN + (step - MAIN), 1)
+        extra_sum[...] += dot(put, value[main:])
+
+    @pl.when(step == 2 * MAIN)
+    def _():
+        partial[...] = extra_sum[...].astype(bf16)
+
+
+def expert_block(z, wg, wu, wd):
+    f32, bf16 = jnp.float32, jnp.bfloat16
+    rows2, packed = z.shape
+    width, units = wg.shape
+    piece = width // MAIN
+    main = rows2 // 2
+    rows = main // MAIN * CAP
+
+    def forth(i):
+        return jnp.minimum(i, MAIN - 1)
+
+    def both(i):
+        return jnp.where(i < MAIN, i, jnp.minimum(i - MAIN, MAIN - 1))
+
+    def after(i):
+        return jnp.maximum(i - MAIN, 0)
+
+    wide = pl.BlockSpec((rows, piece), lambda i: (0, forth(i)))
+    whole = pl.BlockSpec((rows, units), lambda i: (0, 0))
+    sums = pltpu.VMEM((rows, units), f32)
+    hidden = jax.ShapeDtypeStruct((rows, units), bf16)
+    tall = jax.ShapeDtypeStruct((rows, width), bf16)
+    return pl.pallas_call(
+        expert_kernel,
+        grid=(2 * MAIN + 1,),
+        in_specs=[
+            pl.BlockSpec((rows2, piece), lambda i: (0, forth(i))),
+            pl.BlockSpec((rows2, piece), lambda i: (0, MAIN)),
+            pl.BlockSpec((piece, units), lambda i: (both(i), 0)),
+            pl.BlockSpec((piece, units), lambda i: (both(i), 0)),
+            pl.BlockSpec((units, piece), lambda i: (0, forth(i))),
+        ],
+        out_specs=[wide, wide, whole, whole, whole]
+        + [pl.BlockSpec((main, piece), lambda i: (0, after(i)))],
+        out_shape=[tall, tall, hidden, hidden, hidden]
+        + [jax.ShapeDtypeStruct((main, packed), bf16)],
+        scratch_shapes=[sums, sums, sums, pltpu.VMEM((main, piece), f32)],
+        compiler_params=pltpu.CompilerParams(vmem_limit_bytes=48 * 1024 * 1024),
+        cost_estimate=pl.CostEstimate(
+            flops=10 * rows * width * units,
+            bytes_accessed=10 * width * units + 12 * rows * width,
+            transcendentals=rows * units,
+        ),
+    )(z, z, wg, wu, wd)
 
 
 def pack(rows):
@@ -89,55 +191,76 @@
     along_y = lax.rem(me + 2, DP)
     half = send.shape[2] // 2
     first, last = pl.ds(0, half), pl.ds(half, half)
+    side_size = experts // 2
+    side, low = lax.div(pe, side_size), lax.rem(pe, side_size)
+
+    def other(cross, turn):
+        base = (1 - side if cross else side) * side_size
+        return base + lax.rem(low + turn, side_size)
+
+    near = [(0, q) for q in range(1, side_size)]
+    far = [(1, q) for q in range(side_size)]
+    order = [(0, 0)]
+    for i in range(side_size):
+        order += near[i : i + 1] + far[i : i + 1]
     enter(me, pe, experts, (along_x, along_y))
     own = pltpu.make_async_copy(send.at[pe], got.at[0, pe], own_sem)
-    own.start()
-    order = visit_order(experts)
-    across = {}
-    for k in order[1:]:
-        to = lax.rem(pe + k, experts)
-        across[k] = remote(send.at[to], got.at[0, pe], z_sem, k, (me, to))
-        across[k].start()
+    across, sent = {}, []
+    for c, q in near + far:
+        to = other(c, q)
+        across[c, q] = remote(send.at[to], got.at[0, pe], z_sem, c * side_size + q, (me, to))
+    at_once = 2
+    for item in far[:at_once] + near:
+        across[item].start()
+    waiting = far[at_once:]
     copies = {}
     for step in range(experts + 1):
         if step < experts:
-            k = order[step]
-            block = lax.rem(pe + experts - k, experts)
-            if k == 0:
+            c, q = item = order[step]
+            slot = c * side_size + q
+            block = other(c, side_size - q)
+            if step == 0:
                 source = send.at[pe]
             else:
-                across[k].wait_recv()
+                across[item].wait_recv()
                 source = got.at[0, block]
             ways = (
-                remote(source, got.at[1, block], x_sem, k, (along_x, pe)),
-                remote(source, got.at[2, block], y_sem, k, (along_y, pe)),
+                remote(source, got.at[1, block], x_sem, slot, (along_x, pe)),
+                remote(source, got.at[2, block], y_sem, slot, (along_y, pe)),
             )
             for way in ways:
                 way.start()
-            copies[k] = list(ways)
+            copies[item] = list(ways)
+            if step == 0:
+                own.start()
+            if c == 1 and waiting:
+                across[item].wait_send()
+                sent.append(item)
+                across[waiting.pop(0)].start()
         if step >= 1:
-            k = order[step - 1]
-            block = lax.rem(pe + experts - k, experts)
-            copies[k][0].wait_recv()
+            c, q = item = order[step - 1]
+            slot = c * side_size + q
+            block = other(c, side_size - q)
+            copies[item][0].wait_recv()
             onward = remote(
-                got.at[1, block, :, first], got.at[3, block, :, first], xy_sem, k, (along_y, pe)
+                got.at[1, block, :, first], got.at[3, block, :, first], xy_sem, slot, (along_y, pe)
             )
             onward.start()
-            copies[k].append(onward)
-            copies[k][1].wait_recv()
+            copies[item].append(onward)
+            copies[item][1].wait_recv()
             onward = remote(
-                got.at[2, block, :, last], got.at[3, block, :, last], yx_sem, k, (along_x, pe)
+                got.at[2, block, :, last], got.at[3, block, :, last], yx_sem, slot, (along_x, pe)
             )
             onward.start()
-            copies[k].append(onward)
+            copies[item].append(onward)
     own.wait()
-    for k in order:
-        if k != 0:
-            across[k].wait_send()
-        for copy in copies[k]:
+    for item in order:
+        if item != (0, 0) and item not in sent:
+            across[item].wait_send()
+        for copy in copies[item]:
             copy.wait_send()
-        copies[k][2].wait_recv()
-        copies[k][3].wait_recv()
+        copies[item][2].wait_recv()
+        copies[item][3].wait_recv()
 
 
 def dispatch(send):
@@ -211,21 +334,9 @@
     send_dy = jnp.dot(scaled, out_grad.astype(f32), precision=lax.Precision.HIGHEST).astype(bf16)
     both = [pack(rows).reshape(experts, MAIN, -1) for rows in (send_x, send_dy)]
     got = dispatch(jnp.concatenate(both, axis=1))
-    slot_x = unpack(got[:, :, :MAIN].reshape(DP * experts * MAIN, -1), width)
-    slot_dy = unpack(got[:, :, MAIN:].reshape(DP * experts * MAIN, -1), width)
-    wg = w_gate[0]
-    wu = w_up[0]
-    wd = w_down[0]
-    gate = jnp.dot(slot_x, wg, preferred_element_type=f32)
-    up = jnp.dot(slot_x, wu, preferred_element_type=f32)
-    sig = jax.nn.sigmoid(gate)
-    act = (gate * sig * up).astype(bf16)
-    d_act = lax.dot_general(slot_dy, wd, OVER_UNITS, preferred_element_type=f32)
-    d_up = (d_act * gate * sig).astype(bf16)
-    d_gate = (d_act * up * sig * (1.0 + gate * (1.0 - sig))).astype(bf16)
-    partial = lax.dot_general(d_gate, wg, OVER_UNITS, preferred_element_type=f32)
-    partial = partial + lax.dot_general(d_up, wu, OVER_UNITS, preferred_element_type=f32)
-    slot_grad = reduce_to_own(pack(partial.astype(bf16)))
+    z = got.reshape(DP * experts * 2 * MAIN, -1)
+    slot_x, slot_dy, act, d_gate, d_up, partial = expert_block(z, w_gate[0], w_up[0], w_down[0])
+    slot_grad = reduce_to_own(partial)
     gate_grad = lax.dot_general(slot_x, d_gate, OVER_ROWS, preferred_element_type=f32).astype(bf16)
     up_grad = lax.dot_general(slot_x, d_up, OVER_ROWS, preferred_element_type=f32).astype(bf16)
     down_grad = lax.dot_general(act, slot_dy, OVER_ROWS, preferred_element_type=f32).astype(bf16)

time: 134 us -> 131 us (0.978)
  Pallas kernels: 63.8 us -> 89.5 us
  matrix products: 29.2 us -> 13.5 us
  local copies, waits for them, and re-layouts: 17.2 us -> 4.17 us
  waiting for transfers between devices: 10.1 us -> 11.8 us
    pallas_call x0 -> x1, Pallas kernels: none -> 21 us  [expert_block(): pl.pallas_call(expert_kernel, grid=(2 * MAIN + 1,), in_specs=[pl.BlockSpe...]
    dot_general x5 -> x0, matrix products: 13.2 us -> none  [the longest x1 4.26 us: shards(): d_act = lax.dot_general(slot_dy, wd, OVER_UNITS, preferred_element_type=f32)]
    pallas_call x1, Pallas kernels: 46.7 us -> 51.5 us  [dispatch(): pl.pallas_call(functools.partial(dispatch_kernel, experts), out_shape=jax...]
    slice x3 -> x1, local copies, waits for them, and re-layouts: 4.66 us -> 0.28 us  [the longest x1 2.84 us: shards(): slot_dy = unpack(got[:, :, MAIN:].reshape(DP * experts * MAIN, -1), width)]
    slice x3 -> x1, local copies, waits for them, and re-layouts: 4.04 us -> 0.04 us  [unpack(): main = packed[:, :width]]
    reshape x3 -> x1, local copies, waits for them, and re-layouts: 1.93 us -> 0.04 us  [unpack(): extra = packed[:, width:].reshape(packed.shape[0] // MAIN, width)]
    ppermute x4, waiting for transfers between devices: 10.1 us -> 11.8 us  [swap(): return lax.ppermute(value, 'dp', [(i, i ^ bit) for i in range(DP)])]
    unnamed x41 -> x7, local copies, waits for them, and re-layouts: 2.35 us -> 0.95 us
  transfers between devices with their start and end apart: 4 -> 4, of which waited for: 4 -> 3; matrix products, arithmetic and copies ran while one was open for 9% -> 9% of each run, Pallas kernels for 0% -> 0%
where the time goes in v3:
time: 131 us
  Pallas kernels  89.5 us (68%)
  matrix products  13.5 us (10%)
  waiting for transfers between devices  11.8 us (9%)
  other arithmetic  6.55 us (5%)
  starting transfers between devices  4.25 us (3%)
  local copies, waits for them, and re-layouts  4.17 us (3%)
    pallas_call x1, Pallas kernels, dispatch(): pl.pallas_call(functools.partial(dispatch_kernel, experts), out_shape=jax...  51.5 us
    pallas_call x1, Pallas kernels, expert_block(): pl.pallas_call(expert_kernel, grid=(2 * MAIN + 1,), in_specs=[pl.BlockSpe...  21 us
    pallas_call x1, Pallas kernels, exchange(): pl.pallas_call(functools.partial(exchange_kernel, experts), out_shape=jax...  17 us
    ppermute x4, waiting for transfers between devices, swap(): return lax.ppermute(value, 'dp', [(i, i ^ bit) for i in range(DP)])  11.8 us
    ppermute x4, starting transfers between devices, swap(): return lax.ppermute(value, 'dp', [(i, i ^ bit) for i in range(DP)])  4.25 us
    dot_general x1, matrix products, shards(): lax.dot_general(slot_x, d_gate, OVER_ROWS, preferred_element_type=f32)  3.82 us
    dot_general x1, matrix products, shards(): lax.dot_general(slot_x, d_up, OVER_ROWS, preferred_element_type=f32)  3.81 us
    dot_general x1, matrix products, shards(): lax.dot_general(act, slot_dy, OVER_ROWS, preferred_element_type=f32)  3.5 us
  transfers between devices with their start and end apart: 4, of which 3 were waited for; matrix products, arithmetic and copies ran while one was open for 9% of the time, Pallas kernels for 0%

profile of v3, /device:TPU:0, one launch (start us, length us, event | category | flops | bytes accessed | tf_op | source)
XLA Modules:
  0.0 130.6 jit_solution(6550678626710793987)
XLA Ops:
  0.6 0.0 copy-start
  0.6 0.0 copy-start.2
  0.7 0.9 copy.33
  1.6 0.1 eq.43
  1.7 0.1 eq.39
  1.8 2.3 %reduce-window.6 = s32[8,8,128]{2,1,0:T(8,128)S(1)} reduce-window(s32[8,8,128]{2,1,0:T(8,128)S(1)} %fusion.6, s32[]{:T(128)} %constant.3.clone.1), window={size=1x1x128 pad=0_0x0_0x127_0}, to_apply=%region_0.0 | reduce-window | flops 1040384 | bytes 65540 | tf_op jit(solution)/shard_map/reduce-window
  4.1 0.3 slice_reduce_fusion
  4.3 0.2 reduce-window.9
  4.5 0.1 add_bitcast_fusion
  4.6 0.1 reduce_sum.30
  4.8 0.7 select_select_fusion
  5.5 0.9 convert_reduce_fusion
  6.3 0.0 copy-done
  6.3 0.6 convolution_convert_fusion.5
  7.0 0.0 copy-done.2
  7.0 0.3 convolution_convert_fusion.4
  7.3 0.1 slice_bitcast_fusion
  7.5 1.1 maximum_maximum_fusion.send
  8.6 51.5 %shard_map.102 = bf16[4,8,16,4608]{3,2,1,0:T(8,128)(2,1)} custom-call(bf16[8,16,4608]{2,1,0:T(8,128)(2,1)} %maximum_maximum_fusion.send), custom_call_target="tpu_custom_call" | custom-call | bytes 9437184 | tf_op jit(solution)/shard_map/pallas_call | solution.py:270
  60.0 21.0 %shard_map.103 = (bf16[288,4096]{1,0:T(8,128)(2,1)S(1)}, bf16[288,4096]{1,0:T(8,128)(2,1)S(1)}, bf16[288,384]{1,0:T(8,128)(2,1)S(1)}, bf16[288,384]{1,0:T(8,128)...) custom-call(bf16[512,4608]{1,0:T(8,128)(2,1)} %bitcast.50, bf16[512,4608]{1,0:T(8,128)(2,1)} %bitcast.51, ...), custom_call_target="tpu_custom_call" | custom-call | flops 4529848320 | bytes 29884416 | tf_op jit(solution)/shard_map/pallas_call | solution.py:110
  81.0 0.0 copy-start.1
  81.0 1.2 fusion.10
  82.3 0.6 collective-permute-start
  82.9 0.0 copy-done.1
  82.9 1.6 %collective-permute-start.2 = (bf16[128,2304]{1,0:T(8,128)(2,1)S(1)}, bf16[128,2304]{1,0:T(8,128)(2,1)S(1)}, u32[]{:S(2)}, u32[]{:S(2)}) collective-permute-start(bf16[128,2304]{1,0:T(8,128)(2,1)S(1)} %concatenate.46), channel_id=1, source_target_pairs={{0,16},{8,24},{16,0},{24,8},{1,17},{9,25},{17,1},{25,9},{2,18},{10... | collective-permute-start | bytes 1769480 | tf_op jit(solution)/shard_map/ppermute | solution.py:149
  84.5 3.8 %convolution_convert_fusion.2 = bf16[4096,384]{1,0:T(8,128)(2,1)} fusion(bf16[288,4096]{1,0:T(8,128)(2,1)S(1)} %get-tuple-element.15, bf16[288,384]{1,0:T(8,128)(2,1)S(1)} %get-tuple-element.16), kind=kOutput, calls=%fused_computation.2 | convolution fusion | flops 907542528 | bytes 5726208 | tf_op jit(solution)/shard_map/dot_general | solution.py:340
  88.3 7.3 %collective-permute-done = bf16[128,2304]{1,0:T(8,128)(2,1)S(1)} collective-permute-done((bf16[128,2304]{1,0:T(8,128)(2,1)S(1)}, bf16[128,2304]{1,0:T(8,128)(2,1)S(1)}, u32[]{:S(2)}, u32[]{:S(2)}) %collective-permute-start) | collective-permute-done | bytes 589856 | tf_op jit(solution)/shard_map/ppermute | solution.py:149
  95.6 0.1 add_convert_fusion.3
  95.6 1.1 collective-permute-start.1
  96.8 3.8 %convolution_convert_fusion.1 = bf16[4096,384]{1,0:T(8,128)(2,1)} fusion(bf16[288,4096]{1,0:T(8,128)(2,1)S(1)} %get-tuple-element.15, bf16[288,384]{1,0:T(8,128)(2,1)S(1)} %get-tuple-element.17), kind=kOutput, calls=%fused_computation.1 | convolution fusion | flops 907542528 | bytes 5726208 | tf_op jit(solution)/shard_map/dot_general | solution.py:341
  100.6 0.0 collective-permute-done.2
  100.6 2.2 %collective-permute-done.1 = bf16[64,2304]{1,0:T(8,128)(2,1)S(1)} collective-permute-done((bf16[64,2304]{1,0:T(8,128)(2,1)S(1)}, bf16[64,2304]{1,0:T(8,128)(2,1)S(1)}, u32[]{:S(2)}, u32[]{:S(2)}) %collective-permute-start.1) | collective-permute-done | bytes 294944 | tf_op jit(solution)/shard_map/ppermute | solution.py:149
  102.8 0.2 add_convert_fusion.2
  103.0 1.0 collective-permute-start.3
  104.0 3.5 %convolution_convert_fusion = bf16[384,4096]{1,0:T(8,128)(2,1)} fusion(bf16[288,384]{1,0:T(8,128)(2,1)S(1)} %get-tuple-element.18, bf16[288,4096]{1,0:T(8,128)(2,1)S(1)} %get-tuple-element.19), kind=kOutput, calls=%fused_computation | convolution fusion | flops 907542528 | bytes 5726208 | tf_op jit(solution)/shard_map/dot_general | solution.py:342
  107.5 2.3 %collective-permute-done.3 = bf16[64,2304]{1,0:T(8,128)(2,1)S(1)} collective-permute-done((bf16[64,2304]{1,0:T(8,128)(2,1)S(1)}, bf16[64,2304]{1,0:T(8,128)(2,1)S(1)}, u32[]{:S(2)}, u32[]{:S(2)}) %collective-permute-start.3) | collective-permute-done | bytes 294944 | tf_op jit(solution)/shard_map/ppermute | solution.py:149
  109.8 0.1 add_convert_fusion
  110.0 0.9 pad_maximum_fusion.2.send
  110.8 17.0 %shard_map.104 = bf16[8,16,2304]{2,1,0:T(8,128)(2,1)} custom-call(bf16[8,16,2304]{2,1,0:T(8,128)(2,1)} %pad_maximum_fusion.2.send), custom_call_target="tpu_custom_call" | custom-call | bytes 2359296 | tf_op jit(solution)/shard_map/pallas_call | solution.py:299
  127.9 1.1 fusion.11
  129.1 1.4 %convolution_convert_fusion.3 = bf16[128,4096]{1,0:T(8,128)(2,1)} fusion(bf16[8,4096]{1,0:T(8,128)(2,1)S(1)} %reshape.65, bf16[64,4096]{1,0:T(8,128)(2,1)S(1)} %slice.114, bf16[72,128]{1,0:T(8,128)(2,1)S(1)} %get-tuple-element.24), kind=kOutput, calls=%fused_computation.3 | convolution fusion | flops 77201408 | bytes 1656832 | tf_op jit(solution)/shard_map/dot_general | solution.py:351
  (14 shorter events, 0.4 us)
Async XLA Ops:
  0.6 5.7 %copy-start = (bf16[128,4096]{1,0:T(8,128)(2,1)S(1)}, bf16[128,4096]{1,0:T(8,128)(2,1)}, u32[]{:S(2)}) copy-start(bf16[128,4096]{1,0:T(8,128)(2,1)} %param.8) | copy-start | bytes 3145732
  0.6 6.3 %copy-start.2 = (bf16[128,4096]{1,0:T(8,128)(2,1)S(1)}, bf16[128,4096]{1,0:T(8,128)(2,1)}, u32[]{:S(2)}) copy-start(bf16[128,4096]{1,0:T(8,128)(2,1)} %param.7) | copy-start | bytes 3145732
  81.0 1.8 %copy-start.1 = (bf16[256,4608]{1,0:T(8,128)(2,1)S(1)}, bf16[256,4608]{1,0:T(8,128)(2,1)}, u32[]{:S(2)}) copy-start(bf16[256,4608]{1,0:T(8,128)(2,1)} %get-tuple-element.14) | copy-start | bytes 7077892
  82.3 13.3 %collective-permute-start = (bf16[128,2304]{1,0:T(8,128)(2,1)S(1)}, bf16[128,2304]{1,0:T(8,128)(2,1)S(1)}, u32[]{:S(2)}, u32[]{:S(2)}) collective-permute-start(bf16[128,2304]{1,0:T(8,128)(2,1)S(1)} %pad_maximum_fusion), channel_id=1, source_target_pairs={{0,8},{8,0},{16,24},{24,16},{1,9},{9,1},{17,25},{25,17},{2,10},{10... | collective-permute-start | bytes 1769480 | tf_op jit(solution)/shard_map/ppermute | solution.py:149
  82.9 17.7 %collective-permute-start.2 = (bf16[128,2304]{1,0:T(8,128)(2,1)S(1)}, bf16[128,2304]{1,0:T(8,128)(2,1)S(1)}, u32[]{:S(2)}, u32[]{:S(2)}) collective-permute-start(bf16[128,2304]{1,0:T(8,128)(2,1)S(1)} %concatenate.46), channel_id=1, source_target_pairs={{0,16},{8,24},{16,0},{24,8},{1,17},{9,25},{17,1},{25,9},{2,18},{10... | collective-permute-start | bytes 1769480 | tf_op jit(solution)/shard_map/ppermute | solution.py:149
  95.6 7.2 %collective-permute-start.1 = (bf16[64,2304]{1,0:T(8,128)(2,1)S(1)}, bf16[64,2304]{1,0:T(8,128)(2,1)S(1)}, u32[]{:S(2)}, u32[]{:S(2)}) collective-permute-start(bf16[64,2304]{1,0:T(8,128)(2,1)S(1)} %add_convert_fusion.3), channel_id=1, source_target_pairs={{0,16},{8,24},{16,0},{24,8},{1,17},{9,25},{17,1},{25,9},{2,18},{10... | collective-permute-start | bytes 884744 | tf_op jit(solution)/shard_map/ppermute | solution.py:149
  103.0 6.8 %collective-permute-start.3 = (bf16[64,2304]{1,0:T(8,128)(2,1)S(1)}, bf16[64,2304]{1,0:T(8,128)(2,1)S(1)}, u32[]{:S(2)}, u32[]{:S(2)}) collective-permute-start(bf16[64,2304]{1,0:T(8,128)(2,1)S(1)} %get-tuple-element.27), channel_id=1, source_target_pairs={{0,8},{8,0},{16,24},{24,16},{1,9},{9,1},{17,25},{25,17},{2,10},{10... | collective-permute-start | bytes 884744 | tf_op jit(solution)/shard_map/ppermute | solution.py:149

commit v4 on v3

--- a/solution.py
+++ b/solution.py
@@ -145,10 +145,6 @@
     return jnp.concatenate([main, extra], axis=0)
 
 
-def swap(value, bit):
-    return lax.ppermute(value, "dp", [(i, i ^ bit) for i in range(DP)])
-
-
 def visit_order(experts):
     order = [0]
     for k in range(1, experts // 2 + 1):
@@ -191,76 +187,55 @@
     along_y = lax.rem(me + 2, DP)
     half = send.shape[2] // 2
     first, last = pl.ds(0, half), pl.ds(half, half)
-    side_size = experts // 2
-    side, low = lax.div(pe, side_size), lax.rem(pe, side_size)
-
-    def other(cross, turn):
-        base = (1 - side if cross else side) * side_size
-        return base + lax.rem(low + turn, side_size)
-
-    near = [(0, q) for q in range(1, side_size)]
-    far = [(1, q) for q in range(side_size)]
-    order = [(0, 0)]
-    for i in range(side_size):
-        order += near[i : i + 1] + far[i : i + 1]
     enter(me, pe, experts, (along_x, along_y))
     own = pltpu.make_async_copy(send.at[pe], got.at[0, pe], own_sem)
-    across, sent = {}, []
-    for c, q in near + far:
-        to = other(c, q)
-        across[c, q] = remote(send.at[to], got.at[0, pe], z_sem, c * side_size + q, (me, to))
-    at_once = 2
-    for item in far[:at_once] + near:
-        across[item].start()
-    waiting = far[at_once:]
+    own.start()
+    order = visit_order(experts)
+    across = {}
+    for k in order[1:]:
+        to = lax.rem(pe + k, experts)
+        across[k] = remote(send.at[to], got.at[0, pe], z_sem, k, (me, to))
+        across[k].start()
     copies = {}
     for step in range(experts + 1):
         if step < experts:
-            c, q = item = order[step]
-            slot = c * side_size + q
-            block = other(c, side_size - q)
-            if step == 0:
+            k = order[step]
+            block = lax.rem(pe + experts - k, experts)
+            if k == 0:
                 source = send.at[pe]
             else:
-                across[item].wait_recv()
+                across[k].wait_recv()
                 source = got.at[0, block]
             ways = (
-                remote(source, got.at[1, block], x_sem, slot, (along_x, pe)),
-                remote(source, got.at[2, block], y_sem, slot, (along_y, pe)),
+                remote(source, got.at[1, block], x_sem, k, (along_x, pe)),
+                remote(source, got.at[2, block], y_sem, k, (along_y, pe)),
             )
             for way in ways:
                 way.start()
-            copies[item] = list(ways)
-            if step == 0:
-                own.start()
-            if c == 1 and waiting:
-                across[item].wait_send()
-                sent.append(item)
-                across[waiting.pop(0)].start()
+            copies[k] = list(ways)
         if step >= 1:
-            c, q = item = order[step - 1]
-            slot = c * side_size + q
-            block = other(c, side_size - q)
-            copies[item][0].wait_recv()
+            k = order[step - 1]
+            block = lax.rem(pe + experts - k, experts)
+            copies[k][0].wait_recv()
             onward = remote(
-                got.at[1, block, :, first], got.at[3, block, :, first], xy_sem, slot, (along_y, pe)
+                got.at[1, block, :, first], got.at[3, block, :, first], xy_sem, k, (along_y, pe)
             )
             onward.start()
-            copies[item].append(onward)
-            copies[item][1].wait_recv()
+            copies[k].append(onward)
+            copies[k][1].wait_recv()
             onward = remote(
-                got.at[2, block, :, last], got.at[3, block, :, last], yx_sem, slot, (along_x, pe)
+                got.at[2, block, :, last], got.at[3, block, :, last], yx_sem, k, (along_x, pe)
             )
             onward.start()
-            copies[item].append(onward)
+            copies[k].append(onward)
     own.wait()
-    for item in order:
-        if item != (0, 0) and item not in sent:
-            across[item].wait_send()
-        for copy in copies[item]:
+    for k in order:
+        if k != 0:
+            across[k].wait_send()
+        for copy in copies[k]:
             copy.wait_send()
-        copies[item][2].wait_recv()
-        copies[item][3].wait_recv()
+        copies[k][2].wait_recv()
+        copies[k][3].wait_recv()
 
 
 def dispatch(send):
@@ -278,50 +253,89 @@
     )(send)
 
 
-def exchange_kernel(experts, send, got, own_sem, z_sem):
+def return_kernel(
+    experts, chunks, p, got, from_x, from_y, onward, last, ready, own_sem, s1_sem, s2_sem, z_sem
+):
+    f32, bf16 = jnp.float32, jnp.bfloat16
     me, pe = lax.axis_index("dp"), lax.axis_index("expert")
-    enter(me, pe, experts, ())
-    own = pltpu.make_async_copy(send.at[pe], got.at[pe], own_sem)
-    own.start()
-    across = []
-    for k in visit_order(experts)[1:]:
-        to = lax.rem(pe + k, experts)
-        across.append(remote(send.at[to], got.at[pe], z_sem, k, (me, to)))
-        across[-1].start()
-    own.wait()
-    for copy in across:
+    along_x = me + 1 - 2 * lax.rem(me, 2)
+    along_y = lax.rem(me + 2, DP)
+    rows = p.shape[0] // DP
+    wide = p.shape[1] // (2 * chunks)
+    ways = ((along_x, along_y, 1, 2, from_x), (along_y, along_x, 2, 1, from_y))
+
+    def part(r, half, c):
+        return p.at[r * rows : (r + 1) * rows, pl.ds((half * chunks + c) * wide, wide)]
+
+    enter(me, pe, experts, (along_x, along_y))
+    first, second, across, own = {}, {}, [], []
+    for c in range(chunks):
+        for half, (to, _, near, _, land) in enumerate(ways):
+            for i, r in enumerate((3, near)):
+                slot = (c * 2 + half) * 2 + i
+                first[c, half, i] = remote(
+                    part(r, half, c), land.at[c, i], s1_sem, slot, (to, pe)
+                )
+                first[c, half, i].start()
+    for c in range(chunks + 1):
+        if c < chunks:
+            for half, (_, to, _, pass_on, land) in enumerate(ways):
+                first[c, half, 0].wait_recv()
+                value = part(pass_on, half, c)[...].astype(f32) + land[c, 0].astype(f32)
+                onward[c, half] = value.astype(bf16)
+                second[c, half] = remote(
+                    onward.at[c, half], last.at[c, half], s2_sem, c * 2 + half, (to, pe)
+                )
+                second[c, half].start()
+        if c >= 1:
+            d = c - 1
+            totals = []
+            for half, (_, _, _, _, land) in enumerate(ways):
+                first[d, half, 1].wait_recv()
+                second[d, half].wait_recv()
+                total = part(0, half, d)[...].astype(f32) + land[d, 1].astype(f32)
+                total = total + last[d, half].astype(f32)
+                totals.append(total.reshape(experts, MAIN, wide))
+            ready[d] = jnp.concatenate(totals, axis=1).astype(bf16)
+            for k in visit_order(experts)[1:]:
+                to = lax.rem(pe + k, experts)
+                across.append(
+                    remote(ready.at[d, to], got.at[d, pe], z_sem, d * experts + k, (me, to))
+                )
+                across[-1].start()
+            own.append(pltpu.make_async_copy(ready.at[d, pe], got.at[d, pe], own_sem.at[d]))
+            own[-1].start()
+    for copy in list(first.values()) + list(second.values()):
+        copy.wait_send()
+    for copy in own + across:
         copy.wait()
 
 
-def exchange(send):
-    experts = send.shape[0]
-    size = send.size * send.dtype.itemsize
-    return pl.pallas_call(
-        functools.partial(exchange_kernel, experts),
-        out_shape=jax.ShapeDtypeStruct(send.shape, send.dtype),
-        in_specs=[pl.BlockSpec(memory_space=pl.ANY)],
+def return_slots(p, experts):
+    chunks = 2
+    rows, wide = p.shape[0] // DP, p.shape[1] // (2 * chunks)
+    landing = pltpu.VMEM((chunks, 2, rows, wide), p.dtype)
+    size = rows * p.shape[1] * p.dtype.itemsize
+    got = pl.pallas_call(
+        functools.partial(return_kernel, experts, chunks),
+        out_shape=jax.ShapeDtypeStruct((chunks, experts, 2 * MAIN, wide), p.dtype),
+        in_specs=[pl.BlockSpec(memory_space=pltpu.VMEM)],
         out_specs=pl.BlockSpec(memory_space=pl.ANY),
-        scratch_shapes=[pltpu.SemaphoreType.DMA(()), pltpu.SemaphoreType.DMA((2, experts))],
-        compiler_params=pltpu.CompilerParams(collective_id=1, has_side_effects=True),
-        cost_estimate=pl.CostEstimate(flops=0, bytes_accessed=4 * size, transcendentals=0),
-    )(send)
-
-
-def reduce_to_own(parts):
-    rows = parts.shape[0] // DP
-    half = parts.shape[1] // 2
-    f32 = jnp.float32
-    p = [parts[r * rows : (r + 1) * rows] for r in range(DP)]
-
-    def way(cols, first, second):
-        got = swap(jnp.concatenate([p[first][:, cols], p[3][:, cols]], axis=0), first)
-        onward = p[second][:, cols].astype(f32) + got[rows:].astype(f32)
-        last = swap(onward.astype(jnp.bfloat16), second)
-        return p[0][:, cols].astype(f32) + got[:rows].astype(f32) + last.astype(f32)
-
-    a = way(slice(0, half), 1, 2)
-    b = way(slice(half, 2 * half), 2, 1)
-    return jnp.concatenate([a, b], axis=1).astype(jnp.bfloat16)
+        scratch_shapes=[landing] * 4
+        + [
+            pltpu.VMEM((chunks, experts, 2 * MAIN, wide), p.dtype),
+            pltpu.SemaphoreType.DMA((chunks,)),
+            pltpu.SemaphoreType.DMA((2, 4 * chunks)),
+            pltpu.SemaphoreType.DMA((2, 2 * chunks)),
+            pltpu.SemaphoreType.DMA((2, chunks * experts)),
+        ],
+        compiler_params=pltpu.CompilerParams(
+            collective_id=1, has_side_effects=True, vmem_limit_bytes=48 * 1024 * 1024
+        ),
+        cost_estimate=pl.CostEstimate(flops=0, bytes_accessed=8 * size, transcendentals=0),
+    )(p)
+    got = got.reshape(chunks, experts, 2, MAIN, wide).transpose(1, 3, 2, 0, 4)
+    return got.reshape(experts * MAIN, p.shape[1])
 
 
 def shards(tokens, out_grad, expert_ids, gate_weights, w_gate, w_up, w_down):
@@ -336,18 +350,10 @@
     got = dispatch(jnp.concatenate(both, axis=1))
     z = got.reshape(DP * experts * 2 * MAIN, -1)
     slot_x, slot_dy, act, d_gate, d_up, partial = expert_block(z, w_gate[0], w_up[0], w_down[0])
-    slot_grad = reduce_to_own(partial)
+    returned = unpack(return_slots(partial, experts), width)
     gate_grad = lax.dot_general(slot_x, d_gate, OVER_ROWS, preferred_element_type=f32).astype(bf16)
     up_grad = lax.dot_general(slot_x, d_up, OVER_ROWS, preferred_element_type=f32).astype(bf16)
     down_grad = lax.dot_general(act, slot_dy, OVER_ROWS, preferred_element_type=f32).astype(bf16)
-    slot_grad, gate_grad, up_grad, down_grad = lax.optimization_barrier(
-        (slot_grad, gate_grad, up_grad, down_grad)
-    )
-    blocks = slot_grad.reshape(experts, MAIN, -1)
-    half = blocks.shape[2] // 2
-    back = exchange(jnp.concatenate([blocks[:, :, :half], blocks[:, :, half:]], axis=1))
-    back = jnp.concatenate([back[:, :MAIN], back[:, MAIN:]], axis=2)
-    returned = unpack(back.reshape(experts * MAIN, -1), width)
     token_grad = lax.dot_general(place_bf, returned, OVER_ROWS, preferred_element_type=f32)
     return (token_grad.astype(bf16), gate_grad[None], up_grad[None], down_grad[None])
 

time: 131 us -> 139 us (1.061)
  Pallas kernels: 89.5 us -> 103 us
  waiting for transfers between devices: 11.8 us -> 0 us
  local copies, waits for them, and re-layouts: 4.17 us -> 13.2 us
  starting transfers between devices: 4.25 us -> 0 us
  matrix products: 13.5 us -> 16.4 us
    pallas_call x1, Pallas kernels: 17 us -> 35.2 us  [return_slots(): pl.pallas_call(functools.partial(return_kernel, experts, chunks), out_sha...]
    ppermute x4 -> x0, waiting for transfers between devices: 11.8 us -> none  [swap(): return lax.ppermute(value, 'dp', [(i, i ^ bit) for i in range(DP)])]
    unnamed x7 -> x23, local copies, waits for them, and re-layouts: 0.95 us -> 6.09 us
    pallas_call x1, Pallas kernels: 51.5 us -> 46.8 us  [dispatch(): pl.pallas_call(functools.partial(dispatch_kernel, experts), out_shape=jax...]
    ppermute x4 -> x0, starting transfers between devices: 4.25 us -> none  [swap(): return lax.ppermute(value, 'dp', [(i, i ^ bit) for i in range(DP)])]
    reshape x0 -> x2, local copies, waits for them, and re-layouts: none -> 3.67 us  [the longest x1 2.25 us: return_slots(): return got.reshape(experts * MAIN, p.shape[1])]
    slice x4 -> x1, local copies, waits for them, and re-layouts: 2.65 us -> 0.28 us  [the longest x1 1.24 us: way(): p[first][:, cols]]
    slice x1, local copies, waits for them, and re-layouts: 0.04 us -> 1.87 us  [unpack(): main = packed[:, :width]]
  transfers between devices with their start and end apart: 4 -> 0, of which waited for: 3 -> 0; matrix products, arithmetic and copies ran while one was open for 9% -> 0% of each run, Pallas kernels for 0% -> 0%
where the time goes in v4:
time: 139 us; the launch traced here: 138 us
  Pallas kernels  103 us (74%)
  matrix products  16.4 us (12%)
  local copies, waits for them, and re-layouts  13.2 us (9%)
  other arithmetic  5.22 us (4%)
    pallas_call x1, Pallas kernels, dispatch(): pl.pallas_call(functools.partial(dispatch_kernel, experts), out_shape=jax...  46.8 us
    pallas_call x1, Pallas kernels, return_slots(): pl.pallas_call(functools.partial(return_kernel, experts, chunks), out_sha...  35.2 us
    pallas_call x1, Pallas kernels, expert_block(): pl.pallas_call(expert_kernel, grid=(2 * MAIN + 1,), in_specs=[pl.BlockSpe...  21 us
    unnamed x23, local copies, waits for them, and re-layouts  6.09 us
    dot_general x1, matrix products, shards(): lax.dot_general(slot_x, d_gate, OVER_ROWS, preferred_element_type=f32)  5.62 us
    dot_general x1, matrix products, shards(): lax.dot_general(slot_x, d_up, OVER_ROWS, preferred_element_type=f32)  3.82 us
    dot_general x1, matrix products, shards(): lax.dot_general(act, slot_dy, OVER_ROWS, preferred_element_type=f32)  3.5 us

profile of v4, /device:TPU:0, one launch (start us, length us, event | category | flops | bytes accessed | tf_op | source)
XLA Modules:
  0.0 138.5 jit_solution(4804935127361210557)
XLA Ops:
  0.6 0.0 copy-start
  0.6 0.0 copy-start.9
  0.7 0.9 copy.35
  1.6 0.1 eq.43
  1.7 0.1 eq.39
  1.8 2.3 %reduce-window.6 = s32[8,8,128]{2,1,0:T(8,128)S(1)} reduce-window(s32[8,8,128]{2,1,0:T(8,128)S(1)} %fusion.9, s32[]{:T(128)} %constant.3.clone.1), window={size=1x1x128 pad=0_0x0_0x127_0}, to_apply=%region_0.0 | reduce-window | flops 1040384 | bytes 65540 | tf_op jit(solution)/shard_map/reduce-window
  4.1 0.3 slice_reduce_fusion
  4.3 0.2 reduce-window.9
  4.5 0.1 add_bitcast_fusion
  4.6 0.1 reduce_sum.30
  4.8 0.7 select_select_fusion
  5.5 0.9 convert_reduce_fusion
  6.3 0.0 copy-start.10
  6.3 0.0 copy-done
  6.4 0.6 convolution_convert_fusion.5
  7.0 0.0 copy-done.9
  7.0 0.3 convolution_convert_fusion.4
  7.3 0.0 copy-done.10
  7.4 0.1 slice_bitcast_fusion
  7.5 1.1 maximum_maximum_fusion.send
  8.6 46.8 %shard_map.102 = bf16[4,8,16,4608]{3,2,1,0:T(8,128)(2,1)} custom-call(bf16[8,16,4608]{2,1,0:T(8,128)(2,1)} %maximum_maximum_fusion.send), custom_call_target="tpu_custom_call" | custom-call | bytes 9437184 | tf_op jit(solution)/shard_map/pallas_call | solution.py:245
  55.4 21.0 %shard_map.103 = (bf16[288,4096]{1,0:T(8,128)(2,1)S(1)}, bf16[288,4096]{1,0:T(8,128)(2,1)S(1)}, bf16[288,384]{1,0:T(8,128)(2,1)S(1)}, bf16[288,384]{1,0:T(8,128)...) custom-call(bf16[512,4608]{1,0:T(8,128)(2,1)} %bitcast.55, bf16[512,4608]{1,0:T(8,128)(2,1)} %bitcast.56, ...), custom_call_target="tpu_custom_call" | custom-call | flops 4529848320 | bytes 29884416 | tf_op jit(solution)/shard_map/pallas_call | solution.py:110
  76.3 0.0 copy-start.2
  76.3 0.7 copy-done.2
  77.0 0.0 copy-start.4
  77.0 1.4 %copy-done.4 = bf16[288,4096]{1,0:T(8,128)(2,1)} copy-done((bf16[288,4096]{1,0:T(8,128)(2,1)}, bf16[288,4096]{1,0:T(8,128)(2,1)S(1)}, u32[]{:S(2)}) %copy-start.4) | copy-done | bytes 2359320
  78.4 0.0 copy-start.6
  78.4 0.7 copy-done.6
  79.1 0.0 copy-start.8
  79.1 0.7 copy-done.8
  79.8 0.0 copy-start.1
  79.8 1.7 %copy-done.1 = bf16[256,4608]{1,0:T(8,128)(2,1)S(1)} copy-done((bf16[256,4608]{1,0:T(8,128)(2,1)S(1)}, bf16[256,4608]{1,0:T(8,128)(2,1)}, u32[]{:S(2)}) %copy-start.1) | copy-done | bytes 2359320
  81.5 35.2 %shard_map.104 = bf16[2,8,16,1152]{3,2,1,0:T(8,128)(2,1)S(1)} custom-call(bf16[256,4608]{1,0:T(8,128)(2,1)S(1)} %copy-done.1), custom_call_target="tpu_custom_call" | custom-call | bytes 4718592 | tf_op jit(solution)/shard_map/pallas_call | solution.py:319
  116.6 1.4 %copy.47 = bf16[2,8,2,8,1152]{4,0,2,3,1:T(2,128)(2,1)} copy(bf16[2,8,2,8,1152]{4,3,2,1,0:T(8,128)(2,1)S(1)} %bitcast.54) | data formatting | bytes 1179648 | tf_op jit(solution)/shard_map/reshape | solution.py:337
  118.0 2.3 %reshape.64 = bf16[64,4608]{1,0:T(8,128)(2,1)} reshape(bf16[8,8,2,2,1152]{4,3,2,1,0:T(2,128)(2,1)} %bitcast.60) | data formatting | bytes 1179648 | tf_op jit(solution)/shard_map/reshape | solution.py:338
  120.3 0.8 slice.38
  121.1 1.9 %slice.37 = bf16[64,4096]{1,0:T(8,128)(2,1)} slice(bf16[64,4608]{1,0:T(8,128)(2,1)} %reshape.64), slice={[0:64], [0:4096]} | slice | bytes 1048576 | tf_op jit(solution)/shard_map/slice | solution.py:143
  123.0 2.5 %convolution_convert_fusion.3 = bf16[128,4096]{1,0:T(8,128)(2,1)} fusion(bf16[8,4096]{1,0:T(8,128)(2,1)S(1)} %reshape.65, bf16[64,4096]{1,0:T(8,128)(2,1)} %slice.37, bf16[72,128]{1,0:T(8,128)(2,1)} %copy-done.10), kind=kOutput, calls=%fused_computation.6 | convolution fusion | flops 77201408 | bytes 1656832 | tf_op jit(solution)/shard_map/dot_general | solution.py:357
  125.5 0.0 copy-start.5
  125.5 0.0 copy-start.7
  125.5 5.6 %fusion = bf16[1,4096,384]{2,1,0:T(8,128)(2,1)} fusion(bf16[288,4096]{1,0:T(8,128)(2,1)} %copy-done.4, bf16[288,384]{1,0:T(8,128)(2,1)} %copy-done.8), kind=kOutput, calls=%fused_computation.3 | convolution fusion | flops 907542528 | bytes 5726208 | tf_op jit(solution)/shard_map/dot_general | solution.py:354
  131.2 0.0 copy-done.5
  131.2 0.0 copy-done.7
  131.2 0.0 copy-start.3
  131.2 3.8 %fusion.1 = bf16[1,4096,384]{2,1,0:T(8,128)(2,1)} fusion(bf16[288,4096]{1,0:T(8,128)(2,1)S(1)} %copy-done.5, bf16[288,384]{1,0:T(8,128)(2,1)S(1)} %copy-done.7), kind=kOutput, calls=%fused_computation.4 | convolution fusion | flops 907542528 | bytes 5726208 | tf_op jit(solution)/shard_map/dot_general | solution.py:355
  135.0 0.0 copy-done.3
  135.0 3.5 %fusion.2 = bf16[1,384,4096]{2,1,0:T(8,128)(2,1)} fusion(bf16[288,384]{1,0:T(8,128)(2,1)S(1)} %copy-done.3, bf16[288,4096]{1,0:T(8,128)(2,1)S(1)} %get-tuple-element.15), kind=kOutput, calls=%fused_computation.5 | convolution fusion | flops 907542528 | bytes 5726208 | tf_op jit(solution)/shard_map/dot_general | solution.py:356
  (7 shorter events, 0.2 us)
Async XLA Ops:
  0.6 5.7 %copy-start = (bf16[128,4096]{1,0:T(8,128)(2,1)S(1)}, bf16[128,4096]{1,0:T(8,128)(2,1)}, u32[]{:S(2)}) copy-start(bf16[128,4096]{1,0:T(8,128)(2,1)} %param.8) | copy-start | bytes 3145732
  0.6 6.4 %copy-start.9 = (bf16[128,4096]{1,0:T(8,128)(2,1)S(1)}, bf16[128,4096]{1,0:T(8,128)(2,1)}, u32[]{:S(2)}) copy-start(bf16[128,4096]{1,0:T(8,128)(2,1)} %param.7) | copy-start | bytes 3145732
  6.3 1.0 copy-start.10
  76.3 0.7 copy-start.2
  77.0 1.4 %copy-start.4 = (bf16[288,4096]{1,0:T(8,128)(2,1)}, bf16[288,4096]{1,0:T(8,128)(2,1)S(1)}, u32[]{:S(2)}) copy-start(bf16[288,4096]{1,0:T(8,128)(2,1)S(1)} %get-tuple-element.11) | copy-start | bytes 7077892
  78.4 0.7 copy-start.6
  79.1 0.7 copy-start.8
  79.8 1.7 %copy-start.1 = (bf16[256,4608]{1,0:T(8,128)(2,1)S(1)}, bf16[256,4608]{1,0:T(8,128)(2,1)}, u32[]{:S(2)}) copy-start(bf16[256,4608]{1,0:T(8,128)(2,1)} %get-tuple-element.10.p) | copy-start | bytes 7077892
  125.5 5.6 %copy-start.5 = (bf16[288,4096]{1,0:T(8,128)(2,1)S(1)}, bf16[288,4096]{1,0:T(8,128)(2,1)}, u32[]{:S(2)}) copy-start(bf16[288,4096]{1,0:T(8,128)(2,1)} %copy-done.4) | copy-start | bytes 7077892
  125.5 5.6 %copy-start.7 = (bf16[288,384]{1,0:T(8,128)(2,1)S(1)}, bf16[288,384]{1,0:T(8,128)(2,1)}, u32[]{:S(2)}) copy-start(bf16[288,384]{1,0:T(8,128)(2,1)} %copy-done.6) | copy-start | bytes 663556
  131.2 3.8 %copy-start.3 = (bf16[288,384]{1,0:T(8,128)(2,1)S(1)}, bf16[288,384]{1,0:T(8,128)(2,1)}, u32[]{:S(2)}) copy-start(bf16[288,384]{1,0:T(8,128)(2,1)} %copy-done.2) | copy-start | bytes 663556

commit v5 on v3

--- a/solution.py
+++ b/solution.py
@@ -15,17 +15,25 @@
 
 
 def slot_tables(expert_ids, gate_weights, experts):
-    tok_rows, choose = expert_ids.shape
-    flat = expert_ids.reshape(-1)
-    onehot = (flat[:, None] == jnp.arange(experts, dtype=jnp.int32)[None, :]).astype(jnp.int32)
-    before = jnp.cumsum(onehot, axis=0) - onehot
-    ranked = jnp.sum(before * onehot, axis=1)
-    row = jnp.where(ranked < MAIN, flat * MAIN + ranked, experts * MAIN + flat)
-    target = jnp.where(flat < experts, row, -1).reshape(tok_rows, choose)
-    slots = jnp.arange(experts * CAP, dtype=jnp.int32)
-    hits = slots[:, None, None] == target[None, :, :]
-    place = jnp.sum(hits.astype(jnp.float32), axis=2)
-    scaled = jnp.sum(jnp.where(hits, gate_weights[None, :, :], jnp.float32(0.0)), axis=2)
+    tok_rows = expert_ids.shape[0]
+    f32, bf16 = jnp.float32, jnp.bfloat16
+    named = expert_ids.T[None, :, :] == jnp.arange(experts, dtype=jnp.int32)[:, None, None]
+    member = jnp.sum(named.astype(f32), axis=1)
+    weight = jnp.sum(jnp.where(named, gate_weights.T[None, :, :], f32(0.0)), axis=1)
+    token = jnp.arange(tok_rows, dtype=jnp.int32)
+    earlier = (token[:, None] < token[None, :]).astype(bf16)
+    rank = jnp.dot(member.astype(bf16), earlier, preferred_element_type=f32)
+    rank = jnp.where(member > 0, rank, f32(-1.0))
+
+    def spread(values):
+        main = jnp.broadcast_to(values[:, None, :], (experts, MAIN, tok_rows))
+        return jnp.concatenate([main.reshape(experts * MAIN, tok_rows), values], axis=0)
+
+    row = jnp.arange(experts * CAP, dtype=jnp.int32)
+    slot = jnp.where(row < experts * MAIN, row % MAIN, MAIN).astype(f32)
+    hits = spread(rank) == slot[:, None]
+    place = hits.astype(f32)
+    scaled = jnp.where(hits, spread(weight), f32(0.0))
     return (place, scaled)
 
 
@@ -191,76 +199,55 @@
     along_y = lax.rem(me + 2, DP)
     half = send.shape[2] // 2
     first, last = pl.ds(0, half), pl.ds(half, half)
-    side_size = experts // 2
-    side, low = lax.div(pe, side_size), lax.rem(pe, side_size)
-
-    def other(cross, turn):
-        base = (1 - side if cross else side) * side_size
-        return base + lax.rem(low + turn, side_size)
-
-    near = [(0, q) for q in range(1, side_size)]
-    far = [(1, q) for q in range(side_size)]
-    order = [(0, 0)]
-    for i in range(side_size):
-        order += near[i : i + 1] + far[i : i + 1]
     enter(me, pe, experts, (along_x, along_y))
     own = pltpu.make_async_copy(send.at[pe], got.at[0, pe], own_sem)
-    across, sent = {}, []
-    for c, q in near + far:
-        to = other(c, q)
-        across[c, q] = remote(send.at[to], got.at[0, pe], z_sem, c * side_size + q, (me, to))
-    at_once = 2
-    for item in far[:at_once] + near:
-        across[item].start()
-    waiting = far[at_once:]
+    own.start()
+    order = visit_order(experts)
+    across = {}
+    for k in order[1:]:
+        to = lax.rem(pe + k, experts)
+        across[k] = remote(send.at[to], got.at[0, pe], z_sem, k, (me, to))
+        across[k].start()
     copies = {}
     for step in range(experts + 1):
         if step < experts:
-            c, q = item = order[step]
-            slot = c * side_size + q
-            block = other(c, side_size - q)
-            if step == 0:
+            k = order[step]
+            block = lax.rem(pe + experts - k, experts)
+            if k == 0:
                 source = send.at[pe]
             else:
-                across[item].wait_recv()
+                across[k].wait_recv()
                 source = got.at[0, block]
             ways = (
-                remote(source, got.at[1, block], x_sem, slot, (along_x, pe)),
-                remote(source, got.at[2, block], y_sem, slot, (along_y, pe)),
+                remote(source, got.at[1, block], x_sem, k, (along_x, pe)),
+                remote(source, got.at[2, block], y_sem, k, (along_y, pe)),
             )
             for way in ways:
                 way.start()
-            copies[item] = list(ways)
-            if step == 0:
-                own.start()
-            if c == 1 and waiting:
-                across[item].wait_send()
-                sent.append(item)
-                across[waiting.pop(0)].start()
+            copies[k] = list(ways)
         if step >= 1:
-            c, q = item = order[step - 1]
-            slot = c * side_size + q
-            block = other(c, side_size - q)
-            copies[item][0].wait_recv()
+            k = order[step - 1]
+            block = lax.rem(pe + experts - k, experts)
+            copies[k][0].wait_recv()
             onward = remote(
-                got.at[1, block, :, first], got.at[3, block, :, first], xy_sem, slot, (along_y, pe)
+                got.at[1, block, :, first], got.at[3, block, :, first], xy_sem, k, (along_y, pe)
             )
             onward.start()
-            copies[item].append(onward)
-            copies[item][1].wait_recv()
+            copies[k].append(onward)
+            copies[k][1].wait_recv()
             onward = remote(
-                got.at[2, block, :, last], got.at[3, block, :, last], yx_sem, slot, (along_x, pe)
+                got.at[2, block, :, last], got.at[3, block, :, last], yx_sem, k, (along_x, pe)
             )
             onward.start()
-            copies[item].append(onward)
+            copies[k].append(onward)
     own.wait()
-    for item in order:
-        if item != (0, 0) and item not in sent:
-            across[item].wait_send()
-        for copy in copies[item]:
+    for k in order:
+        if k != 0:
+            across[k].wait_send()
+        for copy in copies[k]:
             copy.wait_send()
-        copies[item][2].wait_recv()
-        copies[item][3].wait_recv()
+        copies[k][2].wait_recv()
+        copies[k][3].wait_recv()
 
 
 def dispatch(send):

time: 131 us -> 128 us (0.977)
  waiting for transfers between devices: 11.8 us -> 17.7 us
  Pallas kernels: 89.5 us -> 84.8 us
  other arithmetic: 6.55 us -> 3.39 us
  local copies, waits for them, and re-layouts: 4.17 us -> 2.77 us
    ppermute x4, waiting for transfers between devices: 11.8 us -> 17.7 us  [swap(): return lax.ppermute(value, 'dp', [(i, i ^ bit) for i in range(DP)])]
    pallas_call x1, Pallas kernels: 51.5 us -> 46.8 us  [dispatch(): pl.pallas_call(functools.partial(dispatch_kernel, experts), out_shape=jax...]
    another operation x4 -> x2, other arithmetic: 2.71 us -> 0.28 us
where the time goes in v5:
time: 128 us; the launch traced here: 127 us
  Pallas kernels  84.8 us (66%)
  waiting for transfers between devices  17.7 us (14%)
  matrix products  13.6 us (11%)
  starting transfers between devices  4.07 us (3%)
  other arithmetic  3.39 us (3%)
  local copies, waits for them, and re-layouts  2.77 us (2%)
    pallas_call x1, Pallas kernels, dispatch(): pl.pallas_call(functools.partial(dispatch_kernel, experts), out_shape=jax...  46.8 us
    pallas_call x1, Pallas kernels, expert_block(): pl.pallas_call(expert_kernel, grid=(2 * MAIN + 1,), in_specs=[pl.BlockSpe...  21 us
    ppermute x4, waiting for transfers between devices, swap(): return lax.ppermute(value, 'dp', [(i, i ^ bit) for i in range(DP)])  17.7 us
    pallas_call x1, Pallas kernels, exchange(): pl.pallas_call(functools.partial(exchange_kernel, experts), out_shape=jax...  17 us
    ppermute x4, starting transfers between devices, swap(): return lax.ppermute(value, 'dp', [(i, i ^ bit) for i in range(DP)])  4.07 us
    dot_general x1, matrix products, shards(): lax.dot_general(slot_x, d_gate, OVER_ROWS, preferred_element_type=f32)  3.82 us
    dot_general x1, matrix products, shards(): lax.dot_general(slot_x, d_up, OVER_ROWS, preferred_element_type=f32)  3.81 us
    dot_general x1, matrix products, shards(): lax.dot_general(act, slot_dy, OVER_ROWS, preferred_element_type=f32)  3.5 us
  transfers between devices with their start and end apart: 4, of which 3 were waited for; matrix products, arithmetic and copies ran while one was open for 9% of the time, Pallas kernels for 0%

profile of v5, /device:TPU:0, one launch (start us, length us, event | category | flops | bytes accessed | tf_op | source)
XLA Modules:
  0.0 127.1 jit_solution(13531542028840835435)
XLA Ops:
  0.6 0.0 copy-start
  0.6 0.0 copy-start.2
  0.7 0.9 select_reduce_fusion
  1.5 0.1 convolution_select_fusion
  1.7 0.1 maximum_compare_fusion
  1.8 0.1 copy-done
  1.9 0.6 convolution_convert_fusion.5
  2.5 0.0 copy-done.2
  2.5 0.3 convolution_convert_fusion.4
  2.9 0.1 slice_bitcast_fusion
  3.0 1.1 maximum_maximum_fusion.send
  4.1 46.8 %shard_map.102 = bf16[4,8,16,4608]{3,2,1,0:T(8,128)(2,1)} custom-call(bf16[8,16,4608]{2,1,0:T(8,128)(2,1)} %maximum_maximum_fusion.send), custom_call_target="tpu_custom_call" | custom-call | bytes 9437184 | tf_op jit(solution)/shard_map/pallas_call | solution.py:257
  50.9 21.0 %shard_map.103 = (bf16[288,4096]{1,0:T(8,128)(2,1)S(1)}, bf16[288,4096]{1,0:T(8,128)(2,1)S(1)}, bf16[288,384]{1,0:T(8,128)(2,1)S(1)}, bf16[288,384]{1,0:T(8,128)...) custom-call(bf16[512,4608]{1,0:T(8,128)(2,1)} %bitcast.34, bf16[512,4608]{1,0:T(8,128)(2,1)} %bitcast.35, ...), custom_call_target="tpu_custom_call" | custom-call | flops 4529848320 | bytes 29884416 | tf_op jit(solution)/shard_map/pallas_call | solution.py:118
  71.8 0.0 copy-start.1
  71.8 1.2 fusion.11
  73.1 0.7 collective-permute-start
  73.8 0.0 copy-done.1
  73.9 1.4 %collective-permute-start.2 = (bf16[128,2304]{1,0:T(8,128)(2,1)S(1)}, bf16[128,2304]{1,0:T(8,128)(2,1)S(1)}, u32[]{:S(2)}, u32[]{:S(2)}) collective-permute-start(bf16[128,2304]{1,0:T(8,128)(2,1)S(1)} %concatenate.54), channel_id=1, source_target_pairs={{0,16},{8,24},{16,0},{24,8},{1,17},{9,25},{17,1},{25,9},{2,18},{10... | collective-permute-start | bytes 1769480 | tf_op jit(solution)/shard_map/ppermute | solution.py:157
  75.3 3.8 %convolution_convert_fusion.2 = bf16[4096,384]{1,0:T(8,128)(2,1)} fusion(bf16[288,4096]{1,0:T(8,128)(2,1)S(1)} %get-tuple-element.15, bf16[288,384]{1,0:T(8,128)(2,1)S(1)} %get-tuple-element.16), kind=kOutput, calls=%fused_computation.2 | convolution fusion | flops 907542528 | bytes 5726208 | tf_op jit(solution)/shard_map/dot_general | solution.py:327
  79.1 10.0 %collective-permute-done = bf16[128,2304]{1,0:T(8,128)(2,1)S(1)} collective-permute-done((bf16[128,2304]{1,0:T(8,128)(2,1)S(1)}, bf16[128,2304]{1,0:T(8,128)(2,1)S(1)}, u32[]{:S(2)}, u32[]{:S(2)}) %collective-permute-start) | collective-permute-done | bytes 589856 | tf_op jit(solution)/shard_map/ppermute | solution.py:157
  89.1 0.1 add_convert_fusion.3
  89.2 0.6 collective-permute-start.1
  89.8 3.8 %convolution_convert_fusion.1 = bf16[4096,384]{1,0:T(8,128)(2,1)} fusion(bf16[288,4096]{1,0:T(8,128)(2,1)S(1)} %get-tuple-element.15, bf16[288,384]{1,0:T(8,128)(2,1)S(1)} %get-tuple-element.17), kind=kOutput, calls=%fused_computation.1 | convolution fusion | flops 907542528 | bytes 5726208 | tf_op jit(solution)/shard_map/dot_general | solution.py:328
  93.6 0.0 collective-permute-done.2
  93.6 4.4 %collective-permute-done.1 = bf16[64,2304]{1,0:T(8,128)(2,1)S(1)} collective-permute-done((bf16[64,2304]{1,0:T(8,128)(2,1)S(1)}, bf16[64,2304]{1,0:T(8,128)(2,1)S(1)}, u32[]{:S(2)}, u32[]{:S(2)}) %collective-permute-start.1) | collective-permute-done | bytes 294944 | tf_op jit(solution)/shard_map/ppermute | solution.py:157
  98.0 0.2 add_convert_fusion.2
  98.1 1.3 %collective-permute-start.3 = (bf16[64,2304]{1,0:T(8,128)(2,1)S(1)}, bf16[64,2304]{1,0:T(8,128)(2,1)S(1)}, u32[]{:S(2)}, u32[]{:S(2)}) collective-permute-start(bf16[64,2304]{1,0:T(8,128)(2,1)S(1)} %get-tuple-element.27), channel_id=1, source_target_pairs={{0,8},{8,0},{16,24},{24,16},{1,9},{9,1},{17,25},{25,17},{2,10},{10... | collective-permute-start | bytes 884744 | tf_op jit(solution)/shard_map/ppermute | solution.py:157
  99.5 3.5 %convolution_convert_fusion = bf16[384,4096]{1,0:T(8,128)(2,1)} fusion(bf16[288,384]{1,0:T(8,128)(2,1)S(1)} %get-tuple-element.18, bf16[288,4096]{1,0:T(8,128)(2,1)S(1)} %get-tuple-element.19), kind=kOutput, calls=%fused_computation | convolution fusion | flops 907542528 | bytes 5726208 | tf_op jit(solution)/shard_map/dot_general | solution.py:329
  103.0 3.4 %collective-permute-done.3 = bf16[64,2304]{1,0:T(8,128)(2,1)S(1)} collective-permute-done((bf16[64,2304]{1,0:T(8,128)(2,1)S(1)}, bf16[64,2304]{1,0:T(8,128)(2,1)S(1)}, u32[]{:S(2)}, u32[]{:S(2)}) %collective-permute-start.3) | collective-permute-done | bytes 294944 | tf_op jit(solution)/shard_map/ppermute | solution.py:157
  106.3 0.1 add_convert_fusion
  106.5 0.9 pad_maximum_fusion.2.send
  107.4 17.0 %shard_map.104 = bf16[8,16,2304]{2,1,0:T(8,128)(2,1)} custom-call(bf16[8,16,2304]{2,1,0:T(8,128)(2,1)} %pad_maximum_fusion.2.send), custom_call_target="tpu_custom_call" | custom-call | bytes 2359296 | tf_op jit(solution)/shard_map/pallas_call | solution.py:286
  124.4 1.1 fusion.12
  125.7 1.4 %convolution_convert_fusion.3 = bf16[128,4096]{1,0:T(8,128)(2,1)} fusion(bf16[8,4096]{1,0:T(8,128)(2,1)S(1)} %reshape.58, bf16[64,4096]{1,0:T(8,128)(2,1)S(1)} %slice.105, pred[72,128]{1,0:T(8,128)(4,1)S(1)} %maximum_compare_fusion), kind=kOutput, calls=%fused_computation.3 | convolution fusion | flops 77219840 | bytes 1647616 | tf_op jit(solution)/shard_map/dot_general | solution.py:338
  (14 shorter events, 0.4 us)
Async XLA Ops:
  0.6 1.3 copy-start
  0.6 1.9 %copy-start.2 = (bf16[128,4096]{1,0:T(8,128)(2,1)S(1)}, bf16[128,4096]{1,0:T(8,128)(2,1)}, u32[]{:S(2)}) copy-start(bf16[128,4096]{1,0:T(8,128)(2,1)} %param.7) | copy-start | bytes 3145732
  71.8 2.0 %copy-start.1 = (bf16[256,4608]{1,0:T(8,128)(2,1)S(1)}, bf16[256,4608]{1,0:T(8,128)(2,1)}, u32[]{:S(2)}) copy-start(bf16[256,4608]{1,0:T(8,128)(2,1)} %get-tuple-element.14) | copy-start | bytes 7077892
  73.1 16.0 %collective-permute-start = (bf16[128,2304]{1,0:T(8,128)(2,1)S(1)}, bf16[128,2304]{1,0:T(8,128)(2,1)S(1)}, u32[]{:S(2)}, u32[]{:S(2)}) collective-permute-start(bf16[128,2304]{1,0:T(8,128)(2,1)S(1)} %pad_maximum_fusion), channel_id=1, source_target_pairs={{0,8},{8,0},{16,24},{24,16},{1,9},{9,1},{17,25},{25,17},{2,10},{10... | collective-permute-start | bytes 1769480 | tf_op jit(solution)/shard_map/ppermute | solution.py:157
  73.9 19.7 %collective-permute-start.2 = (bf16[128,2304]{1,0:T(8,128)(2,1)S(1)}, bf16[128,2304]{1,0:T(8,128)(2,1)S(1)}, u32[]{:S(2)}, u32[]{:S(2)}) collective-permute-start(bf16[128,2304]{1,0:T(8,128)(2,1)S(1)} %concatenate.54), channel_id=1, source_target_pairs={{0,16},{8,24},{16,0},{24,8},{1,17},{9,25},{17,1},{25,9},{2,18},{10... | collective-permute-start | bytes 1769480 | tf_op jit(solution)/shard_map/ppermute | solution.py:157
  89.2 8.8 %collective-permute-start.1 = (bf16[64,2304]{1,0:T(8,128)(2,1)S(1)}, bf16[64,2304]{1,0:T(8,128)(2,1)S(1)}, u32[]{:S(2)}, u32[]{:S(2)}) collective-permute-start(bf16[64,2304]{1,0:T(8,128)(2,1)S(1)} %add_convert_fusion.3), channel_id=1, source_target_pairs={{0,16},{8,24},{16,0},{24,8},{1,17},{9,25},{17,1},{25,9},{2,18},{10... | collective-permute-start | bytes 884744 | tf_op jit(solution)/shard_map/ppermute | solution.py:157
  98.1 8.2 %collective-permute-start.3 = (bf16[64,2304]{1,0:T(8,128)(2,1)S(1)}, bf16[64,2304]{1,0:T(8,128)(2,1)S(1)}, u32[]{:S(2)}, u32[]{:S(2)}) collective-permute-start(bf16[64,2304]{1,0:T(8,128)(2,1)S(1)} %get-tuple-element.27), channel_id=1, source_target_pairs={{0,8},{8,0},{16,24},{24,16},{1,9},{9,1},{17,25},{25,17},{2,10},{10... | collective-permute-start | bytes 884744 | tf_op jit(solution)/shard_map/ppermute | solution.py:157

commit v6 on v5

--- a/solution.py
+++ b/solution.py
@@ -44,7 +44,7 @@
 
 
 def expert_kernel(
-    z, z_extra, wg, wu, wd, x, dy, act, d_gate, d_up, partial, gate_sum, up_sum, act_sum, extra_sum
+    z, z_extra, wg, wu, wd, x, dy, act, d_gate, d_up, partial, gate_sum, up_sum, act_sum, extra_sum, picks
 ):
     f32, bf16 = jnp.float32, jnp.bfloat16
     step = pl.program_id(0)
@@ -59,12 +59,15 @@
     def _():
         for total in (gate_sum, up_sum, act_sum):
             total[...] = jnp.zeros_like(total)
+        for i in range(2):
+            picks[i] = one_hot(
+                (main, rows2), lambda r: (r // MAIN) * 2 * MAIN + r % MAIN + i * MAIN
+            )
 
     @pl.when(step < MAIN)
     def _():
         for out, offset in ((x, 0), (dy, MAIN)):
-            pick = one_hot((main, rows2), lambda r: (r // MAIN) * 2 * MAIN + r % MAIN + offset)
-            out[:main, :] = dot(pick, z[...]).astype(bf16)
+            out[:main, :] = dot(picks[offset // MAIN], z[...]).astype(bf16)
             pick = one_hot((blocks, rows2), lambda r: r * 2 * MAIN + offset + step)
             out[main:, :] = dot(pick, z_extra[...]).astype(bf16)
         gate_sum[...] += dot(x[...], wg[...])
@@ -129,7 +132,8 @@
         + [pl.BlockSpec((main, piece), lambda i: (0, after(i)))],
         out_shape=[tall, tall, hidden, hidden, hidden]
         + [jax.ShapeDtypeStruct((main, packed), bf16)],
-        scratch_shapes=[sums, sums, sums, pltpu.VMEM((main, piece), f32)],
+        scratch_shapes=[sums, sums, sums, pltpu.VMEM((main, piece), f32)]
+        + [pltpu.VMEM((2, main, rows2), bf16)],
         compiler_params=pltpu.CompilerParams(vmem_limit_bytes=48 * 1024 * 1024),
         cost_estimate=pl.CostEstimate(
             flops=10 * rows * width * units,

time: 128 us -> 128 us (level)
  no operation moved by 1% of the time
where the time goes in v6:
time: 128 us; the launch traced here: 127 us
  Pallas kernels  84.8 us (66%)
  waiting for transfers between devices  17.7 us (14%)
  matrix products  13.6 us (11%)
  starting transfers between devices  4.08 us (3%)
  other arithmetic  3.39 us (3%)
  local copies, waits for them, and re-layouts  2.77 us (2%)
    pallas_call x1, Pallas kernels, dispatch(): pl.pallas_call(functools.partial(dispatch_kernel, experts), out_shape=jax...  46.8 us
    pallas_call x1, Pallas kernels, expert_block(): pl.pallas_call(expert_kernel, grid=(2 * MAIN + 1,), in_specs=[pl.BlockSpe...  21.1 us
    ppermute x4, waiting for transfers between devices, swap(): return lax.ppermute(value, 'dp', [(i, i ^ bit) for i in range(DP)])  17.7 us
    pallas_call x1, Pallas kernels, exchange(): pl.pallas_call(functools.partial(exchange_kernel, experts), out_shape=jax...  17 us
    ppermute x4, starting transfers between devices, swap(): return lax.ppermute(value, 'dp', [(i, i ^ bit) for i in range(DP)])  4.08 us
    dot_general x1, matrix products, shards(): lax.dot_general(slot_x, d_gate, OVER_ROWS, preferred_element_type=f32)  3.82 us
    dot_general x1, matrix products, shards(): lax.dot_general(slot_x, d_up, OVER_ROWS, preferred_element_type=f32)  3.81 us
    dot_general x1, matrix products, shards(): lax.dot_general(act, slot_dy, OVER_ROWS, preferred_element_type=f32)  3.5 us
  transfers between devices with their start and end apart: 4, of which 3 were waited for; matrix products, arithmetic and copies ran while one was open for 9% of the time, Pallas kernels for 0%

profile of v6, /device:TPU:0, one launch (start us, length us, event | category | flops | bytes accessed | tf_op | source)
XLA Modules:
  0.0 127.2 jit_solution(16197812848334380140)
XLA Ops:
  0.6 0.0 copy-start
  0.6 0.0 copy-start.2
  0.7 0.9 select_reduce_fusion
  1.5 0.1 convolution_select_fusion
  1.7 0.1 maximum_compare_fusion
  1.8 0.1 copy-done
  1.9 0.6 convolution_convert_fusion.5
  2.5 0.0 copy-done.2
  2.5 0.3 convolution_convert_fusion.4
  2.9 0.1 slice_bitcast_fusion
  3.0 1.1 maximum_maximum_fusion.send
  4.1 46.8 %shard_map.102 = bf16[4,8,16,4608]{3,2,1,0:T(8,128)(2,1)} custom-call(bf16[8,16,4608]{2,1,0:T(8,128)(2,1)} %maximum_maximum_fusion.send), custom_call_target="tpu_custom_call" | custom-call | bytes 9437184 | tf_op jit(solution)/shard_map/pallas_call | solution.py:261
  50.9 21.1 %shard_map.103 = (bf16[288,4096]{1,0:T(8,128)(2,1)S(1)}, bf16[288,4096]{1,0:T(8,128)(2,1)S(1)}, bf16[288,384]{1,0:T(8,128)(2,1)S(1)}, bf16[288,384]{1,0:T(8,128)...) custom-call(bf16[512,4608]{1,0:T(8,128)(2,1)} %bitcast.34, bf16[512,4608]{1,0:T(8,128)(2,1)} %bitcast.35, ...), custom_call_target="tpu_custom_call" | custom-call | flops 4529848320 | bytes 29884416 | tf_op jit(solution)/shard_map/pallas_call | solution.py:121
  71.9 0.0 copy-start.1
  71.9 1.2 fusion.11
  73.2 0.7 collective-permute-start
  73.9 0.0 copy-done.1
  74.0 1.4 %collective-permute-start.2 = (bf16[128,2304]{1,0:T(8,128)(2,1)S(1)}, bf16[128,2304]{1,0:T(8,128)(2,1)S(1)}, u32[]{:S(2)}, u32[]{:S(2)}) collective-permute-start(bf16[128,2304]{1,0:T(8,128)(2,1)S(1)} %concatenate.54), channel_id=1, source_target_pairs={{0,16},{8,24},{16,0},{24,8},{1,17},{9,25},{17,1},{25,9},{2,18},{10... | collective-permute-start | bytes 1769480 | tf_op jit(solution)/shard_map/ppermute | solution.py:161
  75.4 3.8 %convolution_convert_fusion.2 = bf16[4096,384]{1,0:T(8,128)(2,1)} fusion(bf16[288,4096]{1,0:T(8,128)(2,1)S(1)} %get-tuple-element.15, bf16[288,384]{1,0:T(8,128)(2,1)S(1)} %get-tuple-element.16), kind=kOutput, calls=%fused_computation.2 | convolution fusion | flops 907542528 | bytes 5726208 | tf_op jit(solution)/shard_map/dot_general | solution.py:331
  79.2 10.0 %collective-permute-done = bf16[128,2304]{1,0:T(8,128)(2,1)S(1)} collective-permute-done((bf16[128,2304]{1,0:T(8,128)(2,1)S(1)}, bf16[128,2304]{1,0:T(8,128)(2,1)S(1)}, u32[]{:S(2)}, u32[]{:S(2)}) %collective-permute-start) | collective-permute-done | bytes 589856 | tf_op jit(solution)/shard_map/ppermute | solution.py:161
  89.2 0.1 add_convert_fusion.3
  89.3 0.6 collective-permute-start.1
  89.9 3.8 %convolution_convert_fusion.1 = bf16[4096,384]{1,0:T(8,128)(2,1)} fusion(bf16[288,4096]{1,0:T(8,128)(2,1)S(1)} %get-tuple-element.15, bf16[288,384]{1,0:T(8,128)(2,1)S(1)} %get-tuple-element.17), kind=kOutput, calls=%fused_computation.1 | convolution fusion | flops 907542528 | bytes 5726208 | tf_op jit(solution)/shard_map/dot_general | solution.py:332
  93.7 0.0 collective-permute-done.2
  93.7 4.3 %collective-permute-done.1 = bf16[64,2304]{1,0:T(8,128)(2,1)S(1)} collective-permute-done((bf16[64,2304]{1,0:T(8,128)(2,1)S(1)}, bf16[64,2304]{1,0:T(8,128)(2,1)S(1)}, u32[]{:S(2)}, u32[]{:S(2)}) %collective-permute-start.1) | collective-permute-done | bytes 294944 | tf_op jit(solution)/shard_map/ppermute | solution.py:161
  98.1 0.2 add_convert_fusion.2
  98.2 1.3 %collective-permute-start.3 = (bf16[64,2304]{1,0:T(8,128)(2,1)S(1)}, bf16[64,2304]{1,0:T(8,128)(2,1)S(1)}, u32[]{:S(2)}, u32[]{:S(2)}) collective-permute-start(bf16[64,2304]{1,0:T(8,128)(2,1)S(1)} %get-tuple-element.27), channel_id=1, source_target_pairs={{0,8},{8,0},{16,24},{24,16},{1,9},{9,1},{17,25},{25,17},{2,10},{10... | collective-permute-start | bytes 884744 | tf_op jit(solution)/shard_map/ppermute | solution.py:161
  99.6 3.5 %convolution_convert_fusion = bf16[384,4096]{1,0:T(8,128)(2,1)} fusion(bf16[288,384]{1,0:T(8,128)(2,1)S(1)} %get-tuple-element.18, bf16[288,4096]{1,0:T(8,128)(2,1)S(1)} %get-tuple-element.19), kind=kOutput, calls=%fused_computation | convolution fusion | flops 907542528 | bytes 5726208 | tf_op jit(solution)/shard_map/dot_general | solution.py:333
  103.1 3.3 %collective-permute-done.3 = bf16[64,2304]{1,0:T(8,128)(2,1)S(1)} collective-permute-done((bf16[64,2304]{1,0:T(8,128)(2,1)S(1)}, bf16[64,2304]{1,0:T(8,128)(2,1)S(1)}, u32[]{:S(2)}, u32[]{:S(2)}) %collective-permute-start.3) | collective-permute-done | bytes 294944 | tf_op jit(solution)/shard_map/ppermute | solution.py:161
  106.4 0.1 add_convert_fusion
  106.6 0.9 pad_maximum_fusion.2.send
  107.5 17.0 %shard_map.104 = bf16[8,16,2304]{2,1,0:T(8,128)(2,1)} custom-call(bf16[8,16,2304]{2,1,0:T(8,128)(2,1)} %pad_maximum_fusion.2.send), custom_call_target="tpu_custom_call" | custom-call | bytes 2359296 | tf_op jit(solution)/shard_map/pallas_call | solution.py:290
  124.5 1.1 fusion.12
  125.7 1.4 %convolution_convert_fusion.3 = bf16[128,4096]{1,0:T(8,128)(2,1)} fusion(bf16[8,4096]{1,0:T(8,128)(2,1)S(1)} %reshape.58, bf16[64,4096]{1,0:T(8,128)(2,1)S(1)} %slice.105, pred[72,128]{1,0:T(8,128)(4,1)S(1)} %maximum_compare_fusion), kind=kOutput, calls=%fused_computation.3 | convolution fusion | flops 77219840 | bytes 1647616 | tf_op jit(solution)/shard_map/dot_general | solution.py:342
  (14 shorter events, 0.4 us)
Async XLA Ops:
  0.6 1.3 copy-start
  0.6 1.9 %copy-start.2 = (bf16[128,4096]{1,0:T(8,128)(2,1)S(1)}, bf16[128,4096]{1,0:T(8,128)(2,1)}, u32[]{:S(2)}) copy-start(bf16[128,4096]{1,0:T(8,128)(2,1)} %param.7) | copy-start | bytes 3145732
  71.9 2.0 %copy-start.1 = (bf16[256,4608]{1,0:T(8,128)(2,1)S(1)}, bf16[256,4608]{1,0:T(8,128)(2,1)}, u32[]{:S(2)}) copy-start(bf16[256,4608]{1,0:T(8,128)(2,1)} %get-tuple-element.14) | copy-start | bytes 7077892
  73.2 16.0 %collective-permute-start = (bf16[128,2304]{1,0:T(8,128)(2,1)S(1)}, bf16[128,2304]{1,0:T(8,128)(2,1)S(1)}, u32[]{:S(2)}, u32[]{:S(2)}) collective-permute-start(bf16[128,2304]{1,0:T(8,128)(2,1)S(1)} %pad_maximum_fusion), channel_id=1, source_target_pairs={{0,8},{8,0},{16,24},{24,16},{1,9},{9,1},{17,25},{25,17},{2,10},{10... | collective-permute-start | bytes 1769480 | tf_op jit(solution)/shard_map/ppermute | solution.py:161
  74.0 19.7 %collective-permute-start.2 = (bf16[128,2304]{1,0:T(8,128)(2,1)S(1)}, bf16[128,2304]{1,0:T(8,128)(2,1)S(1)}, u32[]{:S(2)}, u32[]{:S(2)}) collective-permute-start(bf16[128,2304]{1,0:T(8,128)(2,1)S(1)} %concatenate.54), channel_id=1, source_target_pairs={{0,16},{8,24},{16,0},{24,8},{1,17},{9,25},{17,1},{25,9},{2,18},{10... | collective-permute-start | bytes 1769480 | tf_op jit(solution)/shard_map/ppermute | solution.py:161
  89.3 8.8 %collective-permute-start.1 = (bf16[64,2304]{1,0:T(8,128)(2,1)S(1)}, bf16[64,2304]{1,0:T(8,128)(2,1)S(1)}, u32[]{:S(2)}, u32[]{:S(2)}) collective-permute-start(bf16[64,2304]{1,0:T(8,128)(2,1)S(1)} %add_convert_fusion.3), channel_id=1, source_target_pairs={{0,16},{8,24},{16,0},{24,8},{1,17},{9,25},{17,1},{25,9},{2,18},{10... | collective-permute-start | bytes 884744 | tf_op jit(solution)/shard_map/ppermute | solution.py:161
  98.2 8.2 %collective-permute-start.3 = (bf16[64,2304]{1,0:T(8,128)(2,1)S(1)}, bf16[64,2304]{1,0:T(8,128)(2,1)S(1)}, u32[]{:S(2)}, u32[]{:S(2)}) collective-permute-start(bf16[64,2304]{1,0:T(8,128)(2,1)S(1)} %get-tuple-element.27), channel_id=1, source_target_pairs={{0,8},{8,0},{16,24},{24,16},{1,9},{9,1},{17,25},{25,17},{2,10},{10... | collective-permute-start | bytes 884744 | tf_op jit(solution)/shard_map/ppermute | solution.py:161
